TPU v7x, 512 devices: a whole 4x8x8 slice. The times are simulated.
512 devices in a mesh: rep: 16 (over z, y_lo), gy: 8 (over y_hi, core), gz: 4 (over x).
Axes of the slice: x: 4, y: 8 (y_hi: 4, y_lo: 2; y = y_hi * 2 + y_lo), z: 8, core: 2. Of those that a mesh axis runs over, the one named last changes fastest.
Arguments:
- charges: float32 [4096, 256, 128], P(('rep', 'gz'), 'gy'), may hold values from -6 to 6
- green: float32 [256, 256, 128], P('rep', ('gy', 'gz')), may hold values from 0.1 to 3
Outputs:
- potential: float32 [4096, 256, 128], P(('rep', 'gz'), 'gy')
All inputs are finite; a program needn't handle non-finite values.
Results may differ from a plain program's by a relative error of at most 0.00007.
Values sent between devices are 32-bit elements; how exact they have to be, the bound alone decides.
No kernel may reach another device: no remote copies, remote signals or barrier semaphores. Data moves between devices by JAX's collectives and lax.ppermute only.
A program may use at most 64 MiB of HBM per device.

v0:
```python
import math

import jax
import jax.numpy as jnp
import ml_dtypes
import numpy as np
from jax import lax
from jax.experimental import pallas as pl
from jax.experimental.pallas import tpu as pltpu
from jax.sharding import PartitionSpec as P

NG = 256
NZ = 128
HALF = NZ // 2
GY = 8
GZ = 4
GROUP = GY * GZ
ROWS = NG // GZ
COLS = NG // GY
LANES = 128
LOW = LANES // COLS
HIGH = ROWS // LOW
CHUNK = 4

VMEM_LIMIT = 16 * 1024 * 1024
VMEM_ALL = 60 * 1024 * 1024
F32 = jnp.float32
BF16 = jnp.bfloat16


def parts_of(table, count=2):
    rest = np.asarray(table, np.float64)
    found = []
    for _ in range(count):
        piece = rest.astype(np.float32).astype(ml_dtypes.bfloat16)
        found.append(piece)
        rest = rest - piece.astype(np.float64)
    return found


def depth_tables():
    z = np.arange(NZ)
    there = np.zeros((2, 2, GROUP, NZ))
    back = np.zeros((2, 2, GROUP, NZ))
    for j in range(2):
        for s in range(GROUP):
            k = 2 * s + j
            angle = 2 * math.pi * ((k * z) % NZ) / NZ
            if k == 0:
                there[0, j, s] = 1.0
                there[1, j, s] = 1.0 - 2.0 * (z % 2)
                back[0, j, s] = 1.0
                back[1, j, s] = 2.0 * (z % 2) - 1.0
            else:
                there[0, j, s] = np.cos(angle)
                there[1, j, s] = -np.sin(angle)
                back[0, j, s] = 2 * np.cos(angle)
                back[1, j, s] = 2 * np.sin(angle)
    scale = 1.0 / (NG * NG * NZ)
    return there.reshape(4 * GROUP, NZ), back.reshape(4 * GROUP, NZ) * scale


def row_order():
    low, block, high = np.meshgrid(np.arange(LOW), np.arange(GZ), np.arange(HIGH), indexing="ij")
    return (block * ROWS + high * LOW + low).reshape(-1)


def plane_tables():
    index, order = np.arange(NG), row_order()
    angle = 2 * math.pi * (np.outer(index, index) % NG) / NG
    cos, sin = np.cos(angle), np.sin(angle)
    first = np.concatenate([cos[order][:, order], sin[order][:, order]], axis=1)
    return first, np.concatenate([cos, sin], axis=1)


def pick_table():
    pick = np.zeros((GROUP, 2, 2, NZ))
    for s in range(GROUP):
        for j in range(2):
            k = 2 * s + j
            pick[s, j, 0, k] = 1
            pick[s, j, 1, NZ // 2 if k == 0 else NZ - k] = 1
    return pick.reshape(4 * GROUP, NZ)


def gain_tables():
    index, order = np.arange(NG), row_order()
    place = (order[:, None] == index[None, :]).astype(np.float64)
    opposite = (index[:, None] == (-index[None, :]) % NG).astype(np.float64)
    return np.stack([place, place @ opposite, opposite])


def split2(x):
    high = x.astype(BF16)
    return high, (x - high.astype(F32)).astype(BF16)


def split3(x):
    high = x.astype(BF16)
    rest = x - high.astype(F32)
    mid = rest.astype(BF16)
    return high, mid, (rest - mid.astype(F32)).astype(BF16)


def dot(a, b, da=1, db=0):
    return lax.dot_general(a, b, (((da,), (db,)), ((), ())), preferred_element_type=F32)


def dot3(a, b, da=1, db=0):
    return dot(a[0], b[0], da, db) + (dot(a[0], b[1], da, db) + dot(a[1], b[0], da, db))


def swap_blocks(arrays):
    lane = lax.broadcasted_iota(jnp.int32, arrays[0].shape, 1)
    low_half = lane < 2 * COLS
    even = (lane // COLS) % 2 == 0

    def turn(x, by):
        return pltpu.roll(x, by % LANES, 1)

    x0, x1, x2, x3 = arrays
    y0 = jnp.where(low_half, x0, turn(x2, 2 * COLS))
    y2 = jnp.where(low_half, turn(x0, 2 * COLS), x2)
    y1 = jnp.where(low_half, x1, turn(x3, 2 * COLS))
    y3 = jnp.where(low_half, turn(x1, 2 * COLS), x3)
    z0 = jnp.where(even, y0, turn(y1, COLS))
    z1 = jnp.where(even, turn(y0, -COLS), y1)
    z2 = jnp.where(even, y2, turn(y3, COLS))
    z3 = jnp.where(even, turn(y2, -COLS), y3)
    return z0, z1, z2, z3


def fetch(sources, targets, sems):
    copies = [pltpu.make_async_copy(a, b, sems.at[i]) for i, (a, b) in enumerate(zip(sources, targets, strict=True))]
    for copy in copies:
        copy.start()
    return copies


def wait(copies):
    for copy in copies:
        copy.wait()


def depth_kernel(q_hbm, high_hbm, low_hbm, out_ref, q_ref, w_ref, sems):
    size = CHUNK * LANES
    tables = fetch((high_hbm, low_hbm), (w_ref.at[0], w_ref.at[1]), sems)
    copies = [
        pltpu.make_async_copy(q_hbm.at[i * size : (i + 1) * size], q_ref.at[i * size : (i + 1) * size], sems.at[2 + i])
        for i in range(HIGH // CHUNK)
    ]
    for copy in copies:
        copy.start()
    wait(tables)
    w = (w_ref[0], w_ref[1])
    for h in range(HIGH):
        if h % CHUNK == 0:
            copies[h // CHUNK].wait()
        q = split2(q_ref[h * LANES : (h + 1) * LANES, :])
        t = dot3(w, q, 1, 1)
        for c in range(4):
            out_ref[pl.ds(c * HIGH + h, GROUP, stride=ROWS), :] = t[c * GROUP : (c + 1) * GROUP, :]


def cells_kernel(r_ref, high_ref, low_ref, out_hbm, out_ref, sems):
    w = (high_ref[...], low_ref[...])
    size = CHUNK * LANES
    copies = []
    for h in range(HIGH):
        t = jnp.concatenate([r_ref[pl.ds(c * HIGH + h, GROUP, stride=ROWS), :] for c in range(4)], axis=0)
        out_ref[h * LANES : (h + 1) * LANES, :] = dot3(split2(t.T), w)
        if h % CHUNK == CHUNK - 1:
            i = h // CHUNK
            copies.append(
                pltpu.make_async_copy(out_ref.at[i * size : (i + 1) * size], out_hbm.at[i * size : (i + 1) * size], sems.at[i])
            )
            copies[-1].start()
    wait(copies)


def stacked(high_ref, low_ref, sign):
    def stack(t):
        cos, sin = t[:, :NG], t[:, NG:]
        rows = [[cos, sin], [-sin, cos]] if sign > 0 else [[cos, -sin], [sin, cos]]
        return jnp.concatenate([jnp.concatenate(row, axis=1) for row in rows], axis=0)

    return stack(high_ref[...]), stack(low_ref[...])


def there_kernel(r_ref, lh, ll, rh, rl, out_ref, p_ref):
    for part in range(2):
        for j in range(2):
            c = 2 * part + j
            for gh in range(GY // LOW):
                arrays = [
                    r_ref[(gh * LOW + g) * GZ : (gh * LOW + g + 1) * GZ, c * HIGH : (c + 1) * HIGH, :].reshape(ROWS, LANES)
                    for g in range(LOW)
                ]
                for a, value in enumerate(swap_blocks(arrays)):
                    row, col = part * NG + a * ROWS, j * NG + gh * LANES
                    p_ref[row : row + ROWS, col : col + LANES] = value
    y = dot3(stacked(lh, ll, 1), split2(p_ref[...]))
    y = [jnp.concatenate([y[:NG, j * NG : (j + 1) * NG], y[NG:, j * NG : (j + 1) * NG]], axis=1) for j in range(2)]
    out_ref[...] = dot3(split2(jnp.concatenate(y, axis=0)), stacked(rh, rl, -1))


def back_kernel(f_ref, gain_ref, lh, ll, rh, rl, out_ref):
    columns = []
    for p in range(3):
        rows = slice(p // 2 * NG, (p // 2 + 1) * NG)
        gain = gain_ref[p]
        columns.append(jnp.concatenate([f_ref[rows, :NG] * gain, f_ref[rows, NG:] * -gain], axis=0))
    u = dot3(stacked(lh, ll, 1), split2(jnp.concatenate(columns, axis=1)))
    u = [split2(jnp.concatenate([u[:NG, p * NG : (p + 1) * NG], u[NG:, p * NG : (p + 1) * NG]], axis=1)) for p in range(3)]
    right = stacked(rh, rl, -1)
    v = {(0, 0): dot3(u[0], tuple(t[:, :NG] for t in right)), (1, 0): dot3(u[1], tuple(t[:, NG:] for t in right))}
    both = dot3(u[2], right)
    v[0, 1], v[1, 1] = both[:, :NG], both[:, NG:]
    for (part, j), value in v.items():
        c = 2 * part + j
        for gh in range(GY // LOW):
            arrays = [value[a * ROWS : (a + 1) * ROWS, gh * LANES : (gh + 1) * LANES] for a in range(LOW)]
            for g, cells in enumerate(swap_blocks(arrays)):
                out_ref[(gh * LOW + g) * GZ : (gh * LOW + g + 1) * GZ, c * HIGH : (c + 1) * HIGH, :] = cells.reshape(GZ, HIGH, LANES)


def pick_kernel(g_hbm, pick_hbm, out_ref, g_ref, pick_ref, sems):
    wait(fetch((g_hbm, pick_hbm), (g_ref, pick_ref), sems))
    pick = pick_ref[...]
    chosen = sum(dot(pick, piece, 1, 1) for piece in split3(g_ref[...]))
    for t in range(2):
        out_ref[t * 4 * GROUP : (t + 1) * 4 * GROUP, :] = chosen


def lay_kernel(g_ref, out_ref):
    deep = g_ref.shape[1] // 8
    grow_row = lax.broadcasted_iota(jnp.int32, (GROUP, NG), 0)
    grow_col = lax.broadcasted_iota(jnp.int32, (GROUP, NG), 1)
    grow = (grow_row == grow_col // 8).astype(F32).astype(BF16)
    keep_row = lax.broadcasted_iota(jnp.int32, (deep * 8, NG), 0)
    keep_col = lax.broadcasted_iota(jnp.int32, (deep * 8, NG), 1)
    keep = keep_row % 8 == keep_col % 8
    for t in range(2):
        for p in range(4):
            rows = g_ref[pl.ds(t * 4 * GROUP + p, GROUP, stride=4), :].T
            wide = sum(dot(piece, grow) for piece in split3(rows))
            wide = jnp.where(keep, wide, 0.0)
            out_ref[t, p] = jnp.sum(wide.reshape(deep, 8, NG), axis=1)


def gain_kernel(where_ref, *refs):
    *pieces, table_ref, out_ref, all_ref = refs
    depth, slot = where_ref[0], where_ref[1]
    count = len(pieces)
    deep = NG // (2 * count)
    for step, piece in enumerate(pieces):
        shift = step if step <= count // 2 else step - count
        owner = lax.rem(depth - shift + count, count)
        for t in range(2):
            at = (owner * 2 + t) * deep
            for p in range(4):
                all_ref[p, pl.ds(pl.multiple_of(at, 8), deep), :] = piece[t, p]
    place, opposite_rows, opposite = table_ref[0], table_ref[1], table_ref[2]

    def placed(x):
        return sum(dot(place, piece) for piece in split3(x))

    def reflected(x):
        x = sum(dot(opposite_rows, piece) for piece in split3(x))
        return sum(dot(piece, opposite) for piece in split3(x))

    packed = slot == 0
    own, other = all_ref[0], all_ref[1]
    out_ref[0] = 0.5 * (placed(own) + reflected(jnp.where(packed, own, other)))
    out_ref[1] = 0.5 * (placed(jnp.where(packed, other, own)) + reflected(other))
    out_ref[2] = 0.5 * (placed(all_ref[2]) + reflected(all_ref[3]))


def call(kernel, out_shape, operands, name, flops=0, scratch=(), spaces=None, out_space=pltpu.VMEM, vmem=VMEM_LIMIT):
    moved = sum(x.size * x.dtype.itemsize for x in operands) + math.prod(out_shape) * 4
    spaces = spaces or [pltpu.VMEM] * len(operands)
    return pl.pallas_call(
        kernel,
        out_shape=jax.ShapeDtypeStruct(out_shape, F32),
        in_specs=[pl.BlockSpec(memory_space=space) for space in spaces],
        out_specs=pl.BlockSpec(memory_space=out_space),
        scratch_shapes=list(scratch),
        compiler_params=pltpu.CompilerParams(vmem_limit_bytes=vmem),
        cost_estimate=pl.CostEstimate(flops=flops, bytes_accessed=moved, transcendentals=0),
        name=name,
    )(*operands)


def gains(green):
    depth_count = lax.axis_size("z")
    deep = green.shape[0]
    slot = lax.axis_index("gy") * GZ + lax.axis_index("gz")
    pick = jnp.asarray(pick_table().astype(ml_dtypes.bfloat16))
    sent = call(
        pick_kernel,
        (2 * 4 * GROUP, deep * 8),
        (green.reshape(deep * 8, NZ), pick),
        "pick",
        flops=6 * 128**3,
        spaces=[pltpu.HBM] * 2,
        vmem=VMEM_ALL,
        scratch=[pltpu.VMEM((deep * 8, NZ), F32), pltpu.VMEM((4 * GROUP, NZ), BF16), pltpu.SemaphoreType.DMA((2,))],
    )
    sent = sent.reshape(2 * GROUP, 4, deep * 8)
    got = lax.all_to_all(sent, ("y_lo", "gy", "gz"), split_axis=0, concat_axis=0, tiled=True)
    pair = call(lay_kernel, (2, 4, deep, NG), (got.reshape(2 * 4 * GROUP, deep * 8),), "lay", flops=48 * 128 * 32 * 256)
    def along(value, by):
        return lax.ppermute(value, "z", [(i, (i + by) % depth_count) for i in range(depth_count)])

    from_ = {0: pair, 1: along(pair, 1), -1: along(pair, -1), 2: along(pair, 2), -2: along(pair, -2)}
    from_[3] = along(from_[1], 2)
    from_[-3] = along(from_[-1], -2)
    from_[4] = along(from_[2], 2)
    pieces = [from_[k] for k in (0, 1, 2, 3, 4, -3, -2, -1)]
    where = jnp.stack([lax.axis_index("z"), slot]).astype(jnp.int32)
    selections = jnp.asarray(gain_tables().astype(ml_dtypes.bfloat16))
    return call(
        gain_kernel,
        (3, NG, NG),
        (where, *pieces, selections),
        "gain",
        flops=54 * NG**3,
        scratch=[pltpu.VMEM((4, NG, NG), F32)],
        spaces=[pltpu.SMEM] + [pltpu.VMEM] * 9,
    )


def on_device(charges, green):
    there, back = depth_tables()
    there = [jnp.asarray(t) for t in parts_of(there)]
    back = [jnp.asarray(t) for t in parts_of(back)]
    tables = [jnp.asarray(t) for table in plane_tables() for t in parts_of(table)]
    gain = gains(green)
    cells = ROWS * COLS
    chunks = HIGH // CHUNK
    sent = call(
        depth_kernel,
        (GROUP * ROWS, LANES),
        (charges.reshape(cells, NZ), *there),
        "depth",
        flops=6 * cells * NZ * NZ,
        spaces=[pltpu.HBM] * 3,
        vmem=VMEM_ALL,
        scratch=[pltpu.VMEM((cells, NZ), F32), pltpu.VMEM((2, 4 * GROUP, NZ), BF16), pltpu.SemaphoreType.DMA((2 + chunks,))],
    )
    sent = sent.reshape(GROUP, ROWS, LANES)
    got = lax.all_to_all(sent, ("gy", "gz"), split_axis=0, concat_axis=0, tiled=True)
    spectra = call(
        there_kernel,
        (2 * NG, 2 * NG),
        (got, *tables),
        "there",
        flops=6 * 16 * NG**3,
        scratch=[pltpu.VMEM((2 * NG, 2 * NG), F32)],
    )
    sent = call(
        back_kernel,
        (GROUP, ROWS, LANES),
        (spectra, gain, *tables),
        "back",
        flops=6 * 20 * NG**3,
    )
    got = lax.all_to_all(sent, ("gy", "gz"), split_axis=0, concat_axis=0, tiled=True)
    out = call(
        cells_kernel,
        (cells, NZ),
        (got.reshape(GROUP * ROWS, LANES), *back),
        "cells",
        flops=6 * cells * NZ * NZ,
        scratch=[pltpu.VMEM((cells, NZ), F32), pltpu.SemaphoreType.DMA((chunks,))],
        out_space=pltpu.HBM,
    )
    return out.reshape(charges.shape)


def solution(mesh):
    apart = jax.sharding.Mesh(
        mesh.devices.reshape(mesh.shape["rep"] // 2, 2, mesh.shape["gy"], mesh.shape["gz"]), ("z", "y_lo", "gy", "gz")
    )
    return jax.shard_map(
        on_device,
        mesh=apart,
        in_specs=(P(("z", "y_lo", "gz"), "gy", None), P(("z", "y_lo"), ("gy", "gz"), None)),
        out_specs=P(("z", "y_lo", "gz"), "gy", None),
        check_vma=False,
    )
```

profile of v0, /device:TPU:6, one launch (start us, length us, event | category | flops | bytes accessed | tf_op | source)
XLA Modules:
  0.0 113.1 jit_solution(2453975052783456947)
XLA Ops:
  0.0 1.7 %pick.1 = f32[256,128]{1,0:T(8,128)} custom-call(f32[128,128]{1,0:T(8,128)} %bitcast.14, bf16[128,128]{1,0:T(8,128)(2,1)} %constant.43.clone.pick_hbm), custom_call_target="tpu_custom_call" | custom-call | flops 12582912 | bytes 229376 | tf_op jit(solution)/shard_map/pick/pallas_call | solution.py:282
  1.7 10.6 %all-to-all-start.1 = ((f32[64,4,128]{2,1,0:T(4,128)}), f32[64,4,128]{2,1,0:T(4,128)S(1)}, u32[]{:S(2)}, u32[]{:S(2)}) async-start(f32[64,4,128]{2,1,0:T(4,128)} %bitcast.13), calls=%async_computation.1 | async-start | bytes 262144 | tf_op jit(solution)/shard_map/all_to_all | solution.py:310
  12.3 3.8 %depth.1 = f32[2048,128]{1,0:T(8,128)} custom-call(f32[2048,128]{1,0:T(8,128)} %bitcast.12, bf16[128,128]{1,0:T(8,128)(2,1)} %constant.35.clone.high_hbm, bf16[128,128]{1,0:T(8,128)(2,1)} %constant.36.clone.low_hbm), custom_call_target="tpu_custom_call" | custom-call | flops 201326592 | bytes 2162688 | tf_op jit(solution)/shard_map/depth/pallas_call | solution.py:282
  16.2 5.2 %all-to-all-done.1 = f32[64,4,128]{2,1,0:T(4,128)S(1)} async-done(((f32[64,4,128]{2,1,0:T(4,128)}), f32[64,4,128]{2,1,0:T(4,128)S(1)}, u32[]{:S(2)}, u32[]{:S(2)}) %all-to-all-start.1) | async-done | bytes 131104 | tf_op jit(solution)/shard_map/all_to_all | solution.py:310
  21.4 0.0 copy-start.2
  21.4 5.8 %all-to-all-start = ((f32[32,64,128]{2,1,0:T(8,128)}), f32[32,64,128]{2,1,0:T(8,128)S(1)}, u32[]{:S(2)}, u32[]{:S(2)}) async-start(f32[32,64,128]{2,1,0:T(8,128)} %bitcast.11), calls=%async_computation | async-start | bytes 2097152 | tf_op jit(solution)/shard_map/all_to_all | solution.py:352
  27.2 0.7 lay.1.refs_0_
  27.9 4.3 %collective-permute-start = (f32[2,4,16,256]{3,2,1,0:T(8,128)S(1)}, f32[2,4,16,256]{3,2,1,0:T(8,128)S(1)}, u32[]{:S(2)}, u32[]{:S(2)}) collective-permute-start(f32[2,4,16,256]{3,2,1,0:T(8,128)S(1)} %lay.1.refs_0_), channel_id=1, source_target_pairs={{0,64},{64,128},{128,192},{192,256},{256,320},{320,384},{384,448},... | collective-permute-start | bytes 393224 | tf_op jit(solution)/shard_map/ppermute | solution.py:313
  32.2 6.1 %collective-permute-start.1 = (f32[2,4,16,256]{3,2,1,0:T(8,128)S(1)}, f32[2,4,16,256]{3,2,1,0:T(8,128)S(1)}, u32[]{:S(2)}, u32[]{:S(2)}) collective-permute-start(f32[2,4,16,256]{3,2,1,0:T(8,128)S(1)} %lay.1.refs_0_), channel_id=1, source_target_pairs={{0,128},{64,192},{128,256},{192,320},{256,384},{320,448},{384,0},{... | collective-permute-start | bytes 393224 | tf_op jit(solution)/shard_map/ppermute | solution.py:313
  38.3 4.4 %collective-permute-start.4 = (f32[2,4,16,256]{3,2,1,0:T(8,128)S(1)}, f32[2,4,16,256]{3,2,1,0:T(8,128)S(1)}, u32[]{:S(2)}, u32[]{:S(2)}) collective-permute-start(f32[2,4,16,256]{3,2,1,0:T(8,128)S(1)} %lay.1.refs_0_), channel_id=1, source_target_pairs={{0,448},{64,0},{128,64},{192,128},{256,192},{320,256},{384,320},{4... | collective-permute-start | bytes 393224 | tf_op jit(solution)/shard_map/ppermute | solution.py:313
  42.8 4.8 %collective-permute-start.6 = (f32[2,4,16,256]{3,2,1,0:T(8,128)S(1)}, f32[2,4,16,256]{3,2,1,0:T(8,128)S(1)}, u32[]{:S(2)}, u32[]{:S(2)}) collective-permute-start(f32[2,4,16,256]{3,2,1,0:T(8,128)S(1)} %lay.1.refs_0_), channel_id=1, source_target_pairs={{0,384},{64,448},{128,0},{192,64},{256,128},{320,192},{384,256},{4... | collective-permute-start | bytes 393224 | tf_op jit(solution)/shard_map/ppermute | solution.py:313
  47.6 0.0 collective-permute-done.refs_1_
  47.6 1.9 %collective-permute-start.2 = (f32[2,4,16,256]{3,2,1,0:T(8,128)S(1)}, f32[2,4,16,256]{3,2,1,0:T(8,128)S(1)}, u32[]{:S(2)}, u32[]{:S(2)}) collective-permute-start(f32[2,4,16,256]{3,2,1,0:T(8,128)S(1)} %collective-permute-done.refs_1_), channel_id=1, source_target_pairs={{0,128},{64,192},{128,256},{192,320},{256,384},{320,448},{384,0},{... | collective-permute-start | bytes 393224 | tf_op jit(solution)/shard_map/ppermute | solution.py:313
  49.5 0.0 collective-permute-done.1.refs_2_
  49.5 5.7 %collective-permute-start.3 = (f32[2,4,16,256]{3,2,1,0:T(8,128)S(1)}, f32[2,4,16,256]{3,2,1,0:T(8,128)S(1)}, u32[]{:S(2)}, u32[]{:S(2)}) collective-permute-start(f32[2,4,16,256]{3,2,1,0:T(8,128)S(1)} %collective-permute-done.1.refs_2_), channel_id=1, source_target_pairs={{0,128},{64,192},{128,256},{192,320},{256,384},{320,448},{384,0},{... | collective-permute-start | bytes 393224 | tf_op jit(solution)/shard_map/ppermute | solution.py:313
  55.2 0.0 collective-permute-done.4.refs_7_
  55.2 2.3 %collective-permute-start.5 = (f32[2,4,16,256]{3,2,1,0:T(8,128)S(1)}, f32[2,4,16,256]{3,2,1,0:T(8,128)S(1)}, u32[]{:S(2)}, u32[]{:S(2)}) collective-permute-start(f32[2,4,16,256]{3,2,1,0:T(8,128)S(1)} %collective-permute-done.4.refs_7_), channel_id=1, source_target_pairs={{0,384},{64,448},{128,0},{192,64},{256,128},{320,192},{384,256},{4... | collective-permute-start | bytes 393224 | tf_op jit(solution)/shard_map/ppermute | solution.py:313
  57.5 0.1 pad_add_fusion.where_ref
  57.6 0.0 copy-start.3
  57.6 0.0 copy-start.4
  57.6 0.0 copy-start.5
  57.6 0.0 copy-start.6
  57.6 0.0 collective-permute-done.6.refs_6_
  57.6 3.2 %collective-permute-done.2.refs_3_ = f32[2,4,16,256]{3,2,1,0:T(8,128)S(1)} collective-permute-done((f32[2,4,16,256]{3,2,1,0:T(8,128)S(1)}, f32[2,4,16,256]{3,2,1,0:T(8,128)S(1)}, u32[]{:S(2)}, u32[]{:S(2)}) %collective-permute-start.2) | collective-permute-done | bytes 131104 | tf_op jit(solution)/shard_map/ppermute | solution.py:313
  60.8 4.0 %collective-permute-done.3.refs_4_ = f32[2,4,16,256]{3,2,1,0:T(8,128)S(1)} collective-permute-done((f32[2,4,16,256]{3,2,1,0:T(8,128)S(1)}, f32[2,4,16,256]{3,2,1,0:T(8,128)S(1)}, u32[]{:S(2)}, u32[]{:S(2)}) %collective-permute-start.3) | collective-permute-done | bytes 131104 | tf_op jit(solution)/shard_map/ppermute | solution.py:313
  64.7 0.0 collective-permute-done.5.refs_5_
  64.7 0.0 copy-done.2
  64.7 2.3 %gain.1.gain_ref = f32[3,256,256]{2,1,0:T(8,128)S(1)} custom-call(s32[2]{0:T(128)S(1)} %pad_add_fusion.where_ref, f32[2,4,16,256]{3,2,1,0:T(8,128)S(1)} %lay.1.refs_0_, f32[2,4,16,256]{3,2,1,0:T(8,128)S(1)} %collective-permute-done.refs_1_, f32[2,4,16,256]{3,2,1,0:T(8,128)S(1)} %collective-permute-done.1.refs_2_, ...), custom_call_target="tpu_custom_call" | custom-call | flops 905969664 | bytes 2228232 | tf_op jit(solution)/shard_map/gain/pallas_call | solution.py:282
  67.0 0.0 copy-start.7
  67.1 0.9 copy-done.7
  67.9 0.0 all-to-all-done.r_ref
  67.9 0.0 copy-done.3
  67.9 0.0 copy-done.4
  67.9 0.0 copy-done.5
  68.0 0.0 copy-done.6
  68.0 0.0 copy-start.8
  68.0 2.3 %there.1.f_ref = f32[512,512]{1,0:T(8,128)S(1)} custom-call(f32[32,64,128]{2,1,0:T(8,128)S(1)} %all-to-all-done.r_ref, bf16[256,512]{1,0:T(8,128)(2,1)S(1)} %copy-done.3, bf16[256,512]{1,0:T(8,128)(2,1)S(1)} %copy-done.4, bf16[256,512]{1,0:T(8,128)(2,1)S(1)} %copy-done.5, bf16[256,512]{1,0:T(8,128)(2,1)S(1)} %copy-done.6), custom_call_target="tpu_custom_call" | custom-call | flops 1610612736 | bytes 3145728 | tf_op jit(solution)/shard_map/there/pallas_call | solution.py:282
  70.2 0.0 copy-done.8
  70.2 2.9 %back.1 = f32[32,64,128]{2,1,0:T(8,128)S(1)} custom-call(f32[512,512]{1,0:T(8,128)S(1)} %there.1.f_ref, f32[3,256,256]{2,1,0:T(8,128)S(1)} %copy-done.8, bf16[256,512]{1,0:T(8,128)(2,1)S(1)} %copy-done.3, bf16[256,512]{1,0:T(8,128)(2,1)S(1)} %copy-done.4, bf16[256,512]{1,0:T(8,128)(2,1)S(1)} %copy-done.5, bf16[256,512]{1,0:T(8,128)(2,1)S(1)} %copy-done.6), custom_call_target="tpu_custom_call" | custom-call | flops 2013265920 | bytes 3932160 | tf_op jit(solution)/shard_map/back/pallas_call | solution.py:282
  73.2 0.0 copy-start
  73.2 0.0 copy-start.1
  73.2 38.3 %all_to_all.15 = f32[32,64,128]{2,1,0:T(8,128)S(1)} all-to-all(f32[32,64,128]{2,1,0:T(8,128)S(1)} %back.1), channel_id=1, replica_groups=mesh['z'=8,'y_lo'=2,'gy'=8,'gz'=4] {'gy','gz'}, dimensions={0} | all-to-all | bytes 2097152 | tf_op jit(solution)/shard_map/all_to_all | solution.py:368
  111.5 0.0 copy-done
  111.5 0.0 copy-done.1
  111.5 1.6 %cells.1 = f32[2048,128]{1,0:T(8,128)} custom-call(f32[2048,128]{1,0:T(8,128)S(1)} %bitcast.9, bf16[128,128]{1,0:T(8,128)(2,1)S(1)} %copy-done, bf16[128,128]{1,0:T(8,128)(2,1)S(1)} %copy-done.1), custom_call_target="tpu_custom_call" | custom-call | flops 201326592 | bytes 2162688 | tf_op jit(solution)/shard_map/cells/pallas_call | solution.py:282
Async XLA Ops:
  1.7 19.7 %all-to-all-start.1 = ((f32[64,4,128]{2,1,0:T(4,128)}), f32[64,4,128]{2,1,0:T(4,128)S(1)}, u32[]{:S(2)}, u32[]{:S(2)}) async-start(f32[64,4,128]{2,1,0:T(4,128)} %bitcast.13), calls=%async_computation.1 | async-start | bytes 262144 | tf_op jit(solution)/shard_map/all_to_all | solution.py:310
  21.4 43.3 %copy-start.2 = (bf16[3,256,256]{2,1,0:T(8,128)(2,1)S(1)}, bf16[3,256,256]{2,1,0:T(8,128)(2,1)}, u32[]{:S(2)}) copy-start(bf16[3,256,256]{2,1,0:T(8,128)(2,1)} %constant.44.clone.refs_8_) | copy-start | bytes 1179652
  21.4 46.5 %all-to-all-start = ((f32[32,64,128]{2,1,0:T(8,128)}), f32[32,64,128]{2,1,0:T(8,128)S(1)}, u32[]{:S(2)}, u32[]{:S(2)}) async-start(f32[32,64,128]{2,1,0:T(8,128)} %bitcast.11), calls=%async_computation | async-start | bytes 2097152 | tf_op jit(solution)/shard_map/all_to_all | solution.py:352
  27.9 19.6 %collective-permute-start = (f32[2,4,16,256]{3,2,1,0:T(8,128)S(1)}, f32[2,4,16,256]{3,2,1,0:T(8,128)S(1)}, u32[]{:S(2)}, u32[]{:S(2)}) collective-permute-start(f32[2,4,16,256]{3,2,1,0:T(8,128)S(1)} %lay.1.refs_0_), channel_id=1, source_target_pairs={{0,64},{64,128},{128,192},{192,256},{256,320},{320,384},{384,448},... | collective-permute-start | bytes 393224 | tf_op jit(solution)/shard_map/ppermute | solution.py:313
  32.2 17.3 %collective-permute-start.1 = (f32[2,4,16,256]{3,2,1,0:T(8,128)S(1)}, f32[2,4,16,256]{3,2,1,0:T(8,128)S(1)}, u32[]{:S(2)}, u32[]{:S(2)}) collective-permute-start(f32[2,4,16,256]{3,2,1,0:T(8,128)S(1)} %lay.1.refs_0_), channel_id=1, source_target_pairs={{0,128},{64,192},{128,256},{192,320},{256,384},{320,448},{384,0},{... | collective-permute-start | bytes 393224 | tf_op jit(solution)/shard_map/ppermute | solution.py:313
  38.3 16.9 %collective-permute-start.4 = (f32[2,4,16,256]{3,2,1,0:T(8,128)S(1)}, f32[2,4,16,256]{3,2,1,0:T(8,128)S(1)}, u32[]{:S(2)}, u32[]{:S(2)}) collective-permute-start(f32[2,4,16,256]{3,2,1,0:T(8,128)S(1)} %lay.1.refs_0_), channel_id=1, source_target_pairs={{0,448},{64,0},{128,64},{192,128},{256,192},{320,256},{384,320},{4... | collective-permute-start | bytes 393224 | tf_op jit(solution)/shard_map/ppermute | solution.py:313
  42.8 14.9 %collective-permute-start.6 = (f32[2,4,16,256]{3,2,1,0:T(8,128)S(1)}, f32[2,4,16,256]{3,2,1,0:T(8,128)S(1)}, u32[]{:S(2)}, u32[]{:S(2)}) collective-permute-start(f32[2,4,16,256]{3,2,1,0:T(8,128)S(1)} %lay.1.refs_0_), channel_id=1, source_target_pairs={{0,384},{64,448},{128,0},{192,64},{256,128},{320,192},{384,256},{4... | collective-permute-start | bytes 393224 | tf_op jit(solution)/shard_map/ppermute | solution.py:313
  47.6 13.2 %collective-permute-start.2 = (f32[2,4,16,256]{3,2,1,0:T(8,128)S(1)}, f32[2,4,16,256]{3,2,1,0:T(8,128)S(1)}, u32[]{:S(2)}, u32[]{:S(2)}) collective-permute-start(f32[2,4,16,256]{3,2,1,0:T(8,128)S(1)} %collective-permute-done.refs_1_), channel_id=1, source_target_pairs={{0,128},{64,192},{128,256},{192,320},{256,384},{320,448},{384,0},{... | collective-permute-start | bytes 393224 | tf_op jit(solution)/shard_map/ppermute | solution.py:313
  49.5 15.2 %collective-permute-start.3 = (f32[2,4,16,256]{3,2,1,0:T(8,128)S(1)}, f32[2,4,16,256]{3,2,1,0:T(8,128)S(1)}, u32[]{:S(2)}, u32[]{:S(2)}) collective-permute-start(f32[2,4,16,256]{3,2,1,0:T(8,128)S(1)} %collective-permute-done.1.refs_2_), channel_id=1, source_target_pairs={{0,128},{64,192},{128,256},{192,320},{256,384},{320,448},{384,0},{... | collective-permute-start | bytes 393224 | tf_op jit(solution)/shard_map/ppermute | solution.py:313
  55.2 9.5 %collective-permute-start.5 = (f32[2,4,16,256]{3,2,1,0:T(8,128)S(1)}, f32[2,4,16,256]{3,2,1,0:T(8,128)S(1)}, u32[]{:S(2)}, u32[]{:S(2)}) collective-permute-start(f32[2,4,16,256]{3,2,1,0:T(8,128)S(1)} %collective-permute-done.4.refs_7_), channel_id=1, source_target_pairs={{0,384},{64,448},{128,0},{192,64},{256,128},{320,192},{384,256},{4... | collective-permute-start | bytes 393224 | tf_op jit(solution)/shard_map/ppermute | solution.py:313
  57.6 10.3 %copy-start.3 = (bf16[256,512]{1,0:T(8,128)(2,1)S(1)}, bf16[256,512]{1,0:T(8,128)(2,1)}, u32[]{:S(2)}) copy-start(bf16[256,512]{1,0:T(8,128)(2,1)} %constant.39.clone.lh) | copy-start | bytes 786436
  57.6 10.3 %copy-start.4 = (bf16[256,512]{1,0:T(8,128)(2,1)S(1)}, bf16[256,512]{1,0:T(8,128)(2,1)}, u32[]{:S(2)}) copy-start(bf16[256,512]{1,0:T(8,128)(2,1)} %constant.40.clone.ll) | copy-start | bytes 786436
  57.6 10.3 %copy-start.5 = (bf16[256,512]{1,0:T(8,128)(2,1)S(1)}, bf16[256,512]{1,0:T(8,128)(2,1)}, u32[]{:S(2)}) copy-start(bf16[256,512]{1,0:T(8,128)(2,1)} %constant.41.clone.rh) | copy-start | bytes 786436
  57.6 10.4 %copy-start.6 = (bf16[256,512]{1,0:T(8,128)(2,1)S(1)}, bf16[256,512]{1,0:T(8,128)(2,1)}, u32[]{:S(2)}) copy-start(bf16[256,512]{1,0:T(8,128)(2,1)} %constant.42.clone.rl) | copy-start | bytes 786436
  67.0 0.9 copy-start.7
  68.0 2.3 %copy-start.8 = (f32[3,256,256]{2,1,0:T(8,128)S(1)}, f32[3,256,256]{2,1,0:T(8,128)}, u32[]{:S(2)}) copy-start(f32[3,256,256]{2,1,0:T(8,128)} %copy-done.7) | copy-start | bytes 2359300
  73.2 38.3 %copy-start = (bf16[128,128]{1,0:T(8,128)(2,1)S(1)}, bf16[128,128]{1,0:T(8,128)(2,1)}, u32[]{:S(2)}) copy-start(bf16[128,128]{1,0:T(8,128)(2,1)} %constant.37.clone.high_ref) | copy-start | bytes 98308
  73.2 38.3 %copy-start.1 = (bf16[128,128]{1,0:T(8,128)(2,1)S(1)}, bf16[128,128]{1,0:T(8,128)(2,1)}, u32[]{:S(2)}) copy-start(bf16[128,128]{1,0:T(8,128)(2,1)} %constant.38.clone.low_ref) | copy-start | bytes 98308
where the time goes:
time: 114 us; the launch traced here: 113 us
  starting transfers between devices  45.9 us (40%)
  blocking collectives  38.3 us (34%)
  Pallas kernels  15.3 us (13%)
  waiting for transfers between devices  12.4 us (11%)
    all_to_all x1, blocking collectives, on_device(): lax.all_to_all(sent, ('gy', 'gz'), split_axis=0, concat_axis=0, tiled=True)  38.3 us
    ppermute x7, starting transfers between devices, along(): lax.ppermute(value, 'z', [(i, (i + by) % depth_count) for i in range(dept...  29.5 us
    pallas_call x7, Pallas kernels, call(): pl.pallas_call(kernel, out_shape=jax.ShapeDtypeStruct(out_shape, F32), in...  15.3 us
    all_to_all x1, starting transfers between devices, gains(): lax.all_to_all(sent, ('y_lo', 'gy', 'gz'), split_axis=0, concat_axis=0, t...  10.6 us
    ppermute x7, waiting for transfers between devices, along(): lax.ppermute(value, 'z', [(i, (i + by) % depth_count) for i in range(dept...  7.14 us
    all_to_all x1, starting transfers between devices, on_device(): lax.all_to_all(sent, ('gy', 'gz'), split_axis=0, concat_axis=0, tiled=True)  5.8 us
    all_to_all x1, waiting for transfers between devices, gains(): lax.all_to_all(sent, ('y_lo', 'gy', 'gz'), split_axis=0, concat_axis=0, t...  5.22 us
  transfers between devices with their start and end apart: 9, of which 3 were waited for; matrix products, arithmetic and copies ran while one was open for 0% of the time, Pallas kernels for 6%

commit v1 on v0

--- a/solution.py
+++ b/solution.py
@@ -263,11 +263,11 @@
     place, opposite_rows, opposite = table_ref[0], table_ref[1], table_ref[2]
 
     def placed(x):
-        return sum(dot(place, piece) for piece in split3(x))
+        return sum(dot(place, piece) for piece in split2(x))
 
     def reflected(x):
-        x = sum(dot(opposite_rows, piece) for piece in split3(x))
-        return sum(dot(piece, opposite) for piece in split3(x))
+        x = sum(dot(opposite_rows, piece) for piece in split2(x))
+        return sum(dot(piece, opposite) for piece in split2(x))
 
     packed = slot == 0
     own, other = all_ref[0], all_ref[1]
@@ -291,10 +291,9 @@
     )(*operands)
 
 
-def gains(green):
+def spread(green):
     depth_count = lax.axis_size("z")
     deep = green.shape[0]
-    slot = lax.axis_index("gy") * GZ + lax.axis_index("gz")
     pick = jnp.asarray(pick_table().astype(ml_dtypes.bfloat16))
     sent = call(
         pick_kernel,
@@ -317,6 +316,11 @@
     from_[-3] = along(from_[-1], -2)
     from_[4] = along(from_[2], 2)
     pieces = [from_[k] for k in (0, 1, 2, 3, 4, -3, -2, -1)]
+    return pieces
+
+
+def gains(pieces):
+    slot = lax.axis_index("gy") * GZ + lax.axis_index("gz")
     where = jnp.stack([lax.axis_index("z"), slot]).astype(jnp.int32)
     selections = jnp.asarray(gain_tables().astype(ml_dtypes.bfloat16))
     return call(
@@ -335,7 +339,7 @@
     there = [jnp.asarray(t) for t in parts_of(there)]
     back = [jnp.asarray(t) for t in parts_of(back)]
     tables = [jnp.asarray(t) for table in plane_tables() for t in parts_of(table)]
-    gain = gains(green)
+    pieces = spread(green)
     cells = ROWS * COLS
     chunks = HIGH // CHUNK
     sent = call(
@@ -358,10 +362,11 @@
         flops=6 * 16 * NG**3,
         scratch=[pltpu.VMEM((2 * NG, 2 * NG), F32)],
     )
+    spectra, *pieces[3:6] = lax.optimization_barrier((spectra, *pieces[3:6]))
     sent = call(
         back_kernel,
         (GROUP, ROWS, LANES),
-        (spectra, gain, *tables),
+        (spectra, gains(pieces), *tables),
         "back",
         flops=6 * 20 * NG**3,
     )

time: 114 us -> 110 us (0.965)
  waiting for transfers between devices: 12.4 us -> 10.2 us
    ppermute x7, waiting for transfers between devices: 7.14 us -> 4.93 us  [along(): lax.ppermute(value, 'z', [(i, (i + by) % depth_count) for i in range(dept...]
where the time goes in v1:
time: 110 us
  starting transfers between devices  46 us (42%)
  blocking collectives  38.3 us (35%)
  Pallas kernels  14.9 us (14%)
  waiting for transfers between devices  10.2 us (9%)
    all_to_all x1, blocking collectives, on_device(): lax.all_to_all(sent, ('gy', 'gz'), split_axis=0, concat_axis=0, tiled=True)  38.3 us
    ppermute x7, starting transfers between devices, along(): lax.ppermute(value, 'z', [(i, (i + by) % depth_count) for i in range(dept...  29.6 us
    pallas_call x7, Pallas kernels, call(): pl.pallas_call(kernel, out_shape=jax.ShapeDtypeStruct(out_shape, F32), in...  14.9 us
    all_to_all x1, starting transfers between devices, spread(): lax.all_to_all(sent, ('y_lo', 'gy', 'gz'), split_axis=0, concat_axis=0, t...  10.6 us
    all_to_all x1, starting transfers between devices, on_device(): lax.all_to_all(sent, ('gy', 'gz'), split_axis=0, concat_axis=0, tiled=True)  5.8 us
    all_to_all x1, waiting for transfers between devices, spread(): lax.all_to_all(sent, ('y_lo', 'gy', 'gz'), split_axis=0, concat_axis=0, t...  5.22 us
    ppermute x7, waiting for transfers between devices, along(): lax.ppermute(value, 'z', [(i, (i + by) % depth_count) for i in range(dept...  4.93 us
  transfers between devices with their start and end apart: 9, of which 3 were waited for; matrix products, arithmetic and copies ran while one was open for 0% of the time, Pallas kernels for 6%

profile of v1, /device:TPU:6, one launch (start us, length us, event | category | flops | bytes accessed | tf_op | source)
XLA Modules:
  0.0 109.7 jit_solution(6013435373388356466)
XLA Ops:
  0.0 1.7 %pick.1 = f32[256,128]{1,0:T(8,128)} custom-call(f32[128,128]{1,0:T(8,128)} %bitcast.14, bf16[128,128]{1,0:T(8,128)(2,1)} %constant.43.clone.pick_hbm), custom_call_target="tpu_custom_call" | custom-call | flops 12582912 | bytes 229376 | tf_op jit(solution)/shard_map/pick/pallas_call | solution.py:282
  1.7 10.6 %all-to-all-start.1 = ((f32[64,4,128]{2,1,0:T(4,128)}), f32[64,4,128]{2,1,0:T(4,128)S(1)}, u32[]{:S(2)}, u32[]{:S(2)}) async-start(f32[64,4,128]{2,1,0:T(4,128)} %bitcast.13), calls=%async_computation.1 | async-start | bytes 262144 | tf_op jit(solution)/shard_map/all_to_all | solution.py:309
  12.3 3.8 %depth.1 = f32[2048,128]{1,0:T(8,128)} custom-call(f32[2048,128]{1,0:T(8,128)} %bitcast.12, bf16[128,128]{1,0:T(8,128)(2,1)} %constant.35.clone.high_hbm, bf16[128,128]{1,0:T(8,128)(2,1)} %constant.36.clone.low_hbm), custom_call_target="tpu_custom_call" | custom-call | flops 201326592 | bytes 2162688 | tf_op jit(solution)/shard_map/depth/pallas_call | solution.py:282
  16.2 5.2 %all-to-all-done.1 = f32[64,4,128]{2,1,0:T(4,128)S(1)} async-done(((f32[64,4,128]{2,1,0:T(4,128)}), f32[64,4,128]{2,1,0:T(4,128)S(1)}, u32[]{:S(2)}, u32[]{:S(2)}) %all-to-all-start.1) | async-done | bytes 131104 | tf_op jit(solution)/shard_map/all_to_all | solution.py:309
  21.4 0.0 copy-start.4
  21.4 0.0 copy-start.5
  21.4 0.0 copy-start.6
  21.4 5.8 %all-to-all-start = ((f32[32,64,128]{2,1,0:T(8,128)}), f32[32,64,128]{2,1,0:T(8,128)S(1)}, u32[]{:S(2)}, u32[]{:S(2)}) async-start(f32[32,64,128]{2,1,0:T(8,128)} %bitcast.11), calls=%async_computation | async-start | bytes 2097152 | tf_op jit(solution)/shard_map/all_to_all | solution.py:356
  27.2 0.0 copy-start.3
  27.2 0.7 lay.1.refs_0_
  28.0 4.3 %collective-permute-start = (f32[2,4,16,256]{3,2,1,0:T(8,128)S(1)}, f32[2,4,16,256]{3,2,1,0:T(8,128)S(1)}, u32[]{:S(2)}, u32[]{:S(2)}) collective-permute-start(f32[2,4,16,256]{3,2,1,0:T(8,128)S(1)} %lay.1.refs_0_), channel_id=1, source_target_pairs={{0,64},{64,128},{128,192},{192,256},{256,320},{320,384},{384,448},... | collective-permute-start | bytes 393224 | tf_op jit(solution)/shard_map/ppermute | solution.py:312
  32.2 6.1 %collective-permute-start.2 = (f32[2,4,16,256]{3,2,1,0:T(8,128)S(1)}, f32[2,4,16,256]{3,2,1,0:T(8,128)S(1)}, u32[]{:S(2)}, u32[]{:S(2)}) collective-permute-start(f32[2,4,16,256]{3,2,1,0:T(8,128)S(1)} %lay.1.refs_0_), channel_id=1, source_target_pairs={{0,128},{64,192},{128,256},{192,320},{256,384},{320,448},{384,0},{... | collective-permute-start | bytes 393224 | tf_op jit(solution)/shard_map/ppermute | solution.py:312
  38.3 4.4 %collective-permute-start.4 = (f32[2,4,16,256]{3,2,1,0:T(8,128)S(1)}, f32[2,4,16,256]{3,2,1,0:T(8,128)S(1)}, u32[]{:S(2)}, u32[]{:S(2)}) collective-permute-start(f32[2,4,16,256]{3,2,1,0:T(8,128)S(1)} %lay.1.refs_0_), channel_id=1, source_target_pairs={{0,448},{64,0},{128,64},{192,128},{256,192},{320,256},{384,320},{4... | collective-permute-start | bytes 393224 | tf_op jit(solution)/shard_map/ppermute | solution.py:312
  42.8 0.1 pad_add_fusion.where_ref
  42.9 0.0 copy-start.2
  42.9 4.9 %collective-permute-start.6 = (f32[2,4,16,256]{3,2,1,0:T(8,128)S(1)}, f32[2,4,16,256]{3,2,1,0:T(8,128)S(1)}, u32[]{:S(2)}, u32[]{:S(2)}) collective-permute-start(f32[2,4,16,256]{3,2,1,0:T(8,128)S(1)} %lay.1.refs_0_), channel_id=1, source_target_pairs={{0,384},{64,448},{128,0},{192,64},{256,128},{320,192},{384,256},{4... | collective-permute-start | bytes 393224 | tf_op jit(solution)/shard_map/ppermute | solution.py:312
  47.8 0.0 collective-permute-done.refs_1_
  47.8 1.9 %collective-permute-start.1 = (f32[2,4,16,256]{3,2,1,0:T(8,128)S(1)}, f32[2,4,16,256]{3,2,1,0:T(8,128)S(1)}, u32[]{:S(2)}, u32[]{:S(2)}) collective-permute-start(f32[2,4,16,256]{3,2,1,0:T(8,128)S(1)} %collective-permute-done.refs_1_), channel_id=1, source_target_pairs={{0,128},{64,192},{128,256},{192,320},{256,384},{320,448},{384,0},{... | collective-permute-start | bytes 393224 | tf_op jit(solution)/shard_map/ppermute | solution.py:312
  49.7 0.0 collective-permute-done.2.refs_2_
  49.8 5.7 %collective-permute-start.3 = (f32[2,4,16,256]{3,2,1,0:T(8,128)S(1)}, f32[2,4,16,256]{3,2,1,0:T(8,128)S(1)}, u32[]{:S(2)}, u32[]{:S(2)}) collective-permute-start(f32[2,4,16,256]{3,2,1,0:T(8,128)S(1)} %collective-permute-done.2.refs_2_), channel_id=1, source_target_pairs={{0,128},{64,192},{128,256},{192,320},{256,384},{320,448},{384,0},{... | collective-permute-start | bytes 393224 | tf_op jit(solution)/shard_map/ppermute | solution.py:312
  55.4 0.0 collective-permute-done.4.refs_7_
  55.4 2.3 %collective-permute-start.5 = (f32[2,4,16,256]{3,2,1,0:T(8,128)S(1)}, f32[2,4,16,256]{3,2,1,0:T(8,128)S(1)}, u32[]{:S(2)}, u32[]{:S(2)}) collective-permute-start(f32[2,4,16,256]{3,2,1,0:T(8,128)S(1)} %collective-permute-done.4.refs_7_), channel_id=1, source_target_pairs={{0,384},{64,448},{128,0},{192,64},{256,128},{320,192},{384,256},{4... | collective-permute-start | bytes 393224 | tf_op jit(solution)/shard_map/ppermute | solution.py:312
  57.7 0.0 all-to-all-done.r_ref
  57.7 0.0 copy-done.4
  57.8 0.0 copy-done.5
  57.8 0.0 copy-done.6
  57.8 0.0 copy-done.3
  57.8 2.3 %there.1.f_ref = f32[512,512]{1,0:T(8,128)S(1)} custom-call(f32[32,64,128]{2,1,0:T(8,128)S(1)} %all-to-all-done.r_ref, bf16[256,512]{1,0:T(8,128)(2,1)S(1)} %copy-done.3, bf16[256,512]{1,0:T(8,128)(2,1)S(1)} %copy-done.4, bf16[256,512]{1,0:T(8,128)(2,1)S(1)} %copy-done.5, bf16[256,512]{1,0:T(8,128)(2,1)S(1)} %copy-done.6), custom_call_target="tpu_custom_call" | custom-call | flops 1610612736 | bytes 3145728 | tf_op jit(solution)/shard_map/there/pallas_call | solution.py:282
  60.0 1.0 collective-permute-done.1.refs_3_
  61.0 4.0 %collective-permute-done.3.refs_4_ = f32[2,4,16,256]{3,2,1,0:T(8,128)S(1)} collective-permute-done((f32[2,4,16,256]{3,2,1,0:T(8,128)S(1)}, f32[2,4,16,256]{3,2,1,0:T(8,128)S(1)}, u32[]{:S(2)}, u32[]{:S(2)}) %collective-permute-start.3) | collective-permute-done | bytes 131104 | tf_op jit(solution)/shard_map/ppermute | solution.py:312
  65.0 0.0 collective-permute-done.5.refs_5_
  65.0 0.0 collective-permute-done.6.refs_6_
  65.0 0.0 copy-done.2
  65.0 1.8 %gain.1.gain_ref = f32[3,256,256]{2,1,0:T(8,128)S(1)} custom-call(s32[2]{0:T(128)S(1)} %pad_add_fusion.where_ref, f32[2,4,16,256]{3,2,1,0:T(8,128)S(1)} %lay.1.refs_0_, f32[2,4,16,256]{3,2,1,0:T(8,128)S(1)} %collective-permute-done.refs_1_, f32[2,4,16,256]{3,2,1,0:T(8,128)S(1)} %collective-permute-done.2.refs_2_, ...), custom_call_target="tpu_custom_call" | custom-call | flops 905969664 | bytes 2228232 | tf_op jit(solution)/shard_map/gain/pallas_call | solution.py:282
  66.8 2.9 %back.1 = f32[32,64,128]{2,1,0:T(8,128)S(1)} custom-call(f32[512,512]{1,0:T(8,128)S(1)} %there.1.f_ref, f32[3,256,256]{2,1,0:T(8,128)S(1)} %gain.1.gain_ref, bf16[256,512]{1,0:T(8,128)(2,1)S(1)} %copy-done.3, bf16[256,512]{1,0:T(8,128)(2,1)S(1)} %copy-done.4, bf16[256,512]{1,0:T(8,128)(2,1)S(1)} %copy-done.5, bf16[256,512]{1,0:T(8,128)(2,1)S(1)} %copy-done.6), custom_call_target="tpu_custom_call" | custom-call | flops 2013265920 | bytes 3932160 | tf_op jit(solution)/shard_map/back/pallas_call | solution.py:282
  69.8 0.0 copy-start
  69.8 0.0 copy-start.1
  69.8 38.3 %all_to_all.15 = f32[32,64,128]{2,1,0:T(8,128)S(1)} all-to-all(f32[32,64,128]{2,1,0:T(8,128)S(1)} %back.1), channel_id=1, replica_groups=mesh['z'=8,'y_lo'=2,'gy'=8,'gz'=4] {'gy','gz'}, dimensions={0} | all-to-all | bytes 2097152 | tf_op jit(solution)/shard_map/all_to_all | solution.py:373
  108.1 0.0 copy-done
  108.1 0.0 copy-done.1
  108.1 1.6 %cells.1 = f32[2048,128]{1,0:T(8,128)} custom-call(f32[2048,128]{1,0:T(8,128)S(1)} %bitcast.9, bf16[128,128]{1,0:T(8,128)(2,1)S(1)} %copy-done, bf16[128,128]{1,0:T(8,128)(2,1)S(1)} %copy-done.1), custom_call_target="tpu_custom_call" | custom-call | flops 201326592 | bytes 2162688 | tf_op jit(solution)/shard_map/cells/pallas_call | solution.py:282
Async XLA Ops:
  1.7 19.7 %all-to-all-start.1 = ((f32[64,4,128]{2,1,0:T(4,128)}), f32[64,4,128]{2,1,0:T(4,128)S(1)}, u32[]{:S(2)}, u32[]{:S(2)}) async-start(f32[64,4,128]{2,1,0:T(4,128)} %bitcast.13), calls=%async_computation.1 | async-start | bytes 262144 | tf_op jit(solution)/shard_map/all_to_all | solution.py:309
  21.4 36.3 %copy-start.4 = (bf16[256,512]{1,0:T(8,128)(2,1)S(1)}, bf16[256,512]{1,0:T(8,128)(2,1)}, u32[]{:S(2)}) copy-start(bf16[256,512]{1,0:T(8,128)(2,1)} %constant.40.clone.ll) | copy-start | bytes 786436
  21.4 36.4 %copy-start.5 = (bf16[256,512]{1,0:T(8,128)(2,1)S(1)}, bf16[256,512]{1,0:T(8,128)(2,1)}, u32[]{:S(2)}) copy-start(bf16[256,512]{1,0:T(8,128)(2,1)} %constant.41.clone.rh) | copy-start | bytes 786436
  21.4 36.4 %copy-start.6 = (bf16[256,512]{1,0:T(8,128)(2,1)S(1)}, bf16[256,512]{1,0:T(8,128)(2,1)}, u32[]{:S(2)}) copy-start(bf16[256,512]{1,0:T(8,128)(2,1)} %constant.42.clone.rl) | copy-start | bytes 786436
  21.4 36.3 %all-to-all-start = ((f32[32,64,128]{2,1,0:T(8,128)}), f32[32,64,128]{2,1,0:T(8,128)S(1)}, u32[]{:S(2)}, u32[]{:S(2)}) async-start(f32[32,64,128]{2,1,0:T(8,128)} %bitcast.11), calls=%async_computation | async-start | bytes 2097152 | tf_op jit(solution)/shard_map/all_to_all | solution.py:356
  27.2 30.6 %copy-start.3 = (bf16[256,512]{1,0:T(8,128)(2,1)S(1)}, bf16[256,512]{1,0:T(8,128)(2,1)}, u32[]{:S(2)}) copy-start(bf16[256,512]{1,0:T(8,128)(2,1)} %constant.39.clone.lh) | copy-start | bytes 786436
  28.0 19.8 %collective-permute-start = (f32[2,4,16,256]{3,2,1,0:T(8,128)S(1)}, f32[2,4,16,256]{3,2,1,0:T(8,128)S(1)}, u32[]{:S(2)}, u32[]{:S(2)}) collective-permute-start(f32[2,4,16,256]{3,2,1,0:T(8,128)S(1)} %lay.1.refs_0_), channel_id=1, source_target_pairs={{0,64},{64,128},{128,192},{192,256},{256,320},{320,384},{384,448},... | collective-permute-start | bytes 393224 | tf_op jit(solution)/shard_map/ppermute | solution.py:312
  32.2 17.5 %collective-permute-start.2 = (f32[2,4,16,256]{3,2,1,0:T(8,128)S(1)}, f32[2,4,16,256]{3,2,1,0:T(8,128)S(1)}, u32[]{:S(2)}, u32[]{:S(2)}) collective-permute-start(f32[2,4,16,256]{3,2,1,0:T(8,128)S(1)} %lay.1.refs_0_), channel_id=1, source_target_pairs={{0,128},{64,192},{128,256},{192,320},{256,384},{320,448},{384,0},{... | collective-permute-start | bytes 393224 | tf_op jit(solution)/shard_map/ppermute | solution.py:312
  38.3 17.1 %collective-permute-start.4 = (f32[2,4,16,256]{3,2,1,0:T(8,128)S(1)}, f32[2,4,16,256]{3,2,1,0:T(8,128)S(1)}, u32[]{:S(2)}, u32[]{:S(2)}) collective-permute-start(f32[2,4,16,256]{3,2,1,0:T(8,128)S(1)} %lay.1.refs_0_), channel_id=1, source_target_pairs={{0,448},{64,0},{128,64},{192,128},{256,192},{320,256},{384,320},{4... | collective-permute-start | bytes 393224 | tf_op jit(solution)/shard_map/ppermute | solution.py:312
  42.9 22.1 %copy-start.2 = (bf16[3,256,256]{2,1,0:T(8,128)(2,1)S(1)}, bf16[3,256,256]{2,1,0:T(8,128)(2,1)}, u32[]{:S(2)}) copy-start(bf16[3,256,256]{2,1,0:T(8,128)(2,1)} %constant.44.clone.refs_8_) | copy-start | bytes 1179652
  42.9 22.1 %collective-permute-start.6 = (f32[2,4,16,256]{3,2,1,0:T(8,128)S(1)}, f32[2,4,16,256]{3,2,1,0:T(8,128)S(1)}, u32[]{:S(2)}, u32[]{:S(2)}) collective-permute-start(f32[2,4,16,256]{3,2,1,0:T(8,128)S(1)} %lay.1.refs_0_), channel_id=1, source_target_pairs={{0,384},{64,448},{128,0},{192,64},{256,128},{320,192},{384,256},{4... | collective-permute-start | bytes 393224 | tf_op jit(solution)/shard_map/ppermute | solution.py:312
  47.8 13.2 %collective-permute-start.1 = (f32[2,4,16,256]{3,2,1,0:T(8,128)S(1)}, f32[2,4,16,256]{3,2,1,0:T(8,128)S(1)}, u32[]{:S(2)}, u32[]{:S(2)}) collective-permute-start(f32[2,4,16,256]{3,2,1,0:T(8,128)S(1)} %collective-permute-done.refs_1_), channel_id=1, source_target_pairs={{0,128},{64,192},{128,256},{192,320},{256,384},{320,448},{384,0},{... | collective-permute-start | bytes 393224 | tf_op jit(solution)/shard_map/ppermute | solution.py:312
  49.8 15.2 %collective-permute-start.3 = (f32[2,4,16,256]{3,2,1,0:T(8,128)S(1)}, f32[2,4,16,256]{3,2,1,0:T(8,128)S(1)}, u32[]{:S(2)}, u32[]{:S(2)}) collective-permute-start(f32[2,4,16,256]{3,2,1,0:T(8,128)S(1)} %collective-permute-done.2.refs_2_), channel_id=1, source_target_pairs={{0,128},{64,192},{128,256},{192,320},{256,384},{320,448},{384,0},{... | collective-permute-start | bytes 393224 | tf_op jit(solution)/shard_map/ppermute | solution.py:312
  55.4 9.5 %collective-permute-start.5 = (f32[2,4,16,256]{3,2,1,0:T(8,128)S(1)}, f32[2,4,16,256]{3,2,1,0:T(8,128)S(1)}, u32[]{:S(2)}, u32[]{:S(2)}) collective-permute-start(f32[2,4,16,256]{3,2,1,0:T(8,128)S(1)} %collective-permute-done.4.refs_7_), channel_id=1, source_target_pairs={{0,384},{64,448},{128,0},{192,64},{256,128},{320,192},{384,256},{4... | collective-permute-start | bytes 393224 | tf_op jit(solution)/shard_map/ppermute | solution.py:312
  69.8 38.3 %copy-start = (bf16[128,128]{1,0:T(8,128)(2,1)S(1)}, bf16[128,128]{1,0:T(8,128)(2,1)}, u32[]{:S(2)}) copy-start(bf16[128,128]{1,0:T(8,128)(2,1)} %constant.37.clone.high_ref) | copy-start | bytes 98308
  69.8 38.3 %copy-start.1 = (bf16[128,128]{1,0:T(8,128)(2,1)S(1)}, bf16[128,128]{1,0:T(8,128)(2,1)}, u32[]{:S(2)}) copy-start(bf16[128,128]{1,0:T(8,128)(2,1)} %constant.38.clone.low_ref) | copy-start | bytes 98308

commit v2 on v1

--- a/solution.py
+++ b/solution.py
@@ -204,17 +204,26 @@
     out_ref[...] = dot3(split2(jnp.concatenate(y, axis=0)), stacked(rh, rl, -1))
 
 
-def back_kernel(f_ref, gain_ref, lh, ll, rh, rl, out_ref):
+def across(t):
+    return jnp.concatenate([t[0], t[0], t[1]], axis=1)
+
+
+def down(t):
+    return jnp.concatenate([t[0], t[1], t[0]], axis=0)
+
+
+def back_kernel(where_ref, f_ref, early_ref, *refs):
+    *halves, table_ref, lh, ll, rh, rl, out_ref, rows_ref, late_ref = refs
     columns = []
-    for p in range(3):
+    for p, gain in enumerate(late_gains(where_ref, halves, early_ref, table_ref, rows_ref, late_ref)):
         rows = slice(p // 2 * NG, (p // 2 + 1) * NG)
-        gain = gain_ref[p]
         columns.append(jnp.concatenate([f_ref[rows, :NG] * gain, f_ref[rows, NG:] * -gain], axis=0))
-    u = dot3(stacked(lh, ll, 1), split2(jnp.concatenate(columns, axis=1)))
+    u = dot(across(stacked(lh, ll, 1)), down(split2(jnp.concatenate(columns, axis=1))))
     u = [split2(jnp.concatenate([u[:NG, p * NG : (p + 1) * NG], u[NG:, p * NG : (p + 1) * NG]], axis=1)) for p in range(3)]
-    right = stacked(rh, rl, -1)
-    v = {(0, 0): dot3(u[0], tuple(t[:, :NG] for t in right)), (1, 0): dot3(u[1], tuple(t[:, NG:] for t in right))}
-    both = dot3(u[2], right)
+    u = [across(t) for t in u]
+    right = down(stacked(rh, rl, -1))
+    v = {(0, 0): dot(u[0], right[:, :NG]), (1, 0): dot(u[1], right[:, NG:])}
+    both = dot(u[2], right)
     v[0, 1], v[1, 1] = both[:, :NG], both[:, NG:]
     for (part, j), value in v.items():
         c = 2 * part + j
@@ -248,18 +257,15 @@
             out_ref[t, p] = jnp.sum(wide.reshape(deep, 8, NG), axis=1)
 
 
-def gain_kernel(where_ref, *refs):
-    *pieces, table_ref, out_ref, all_ref = refs
-    depth, slot = where_ref[0], where_ref[1]
-    count = len(pieces)
-    deep = NG // (2 * count)
-    for step, piece in enumerate(pieces):
-        shift = step if step <= count // 2 else step - count
-        owner = lax.rem(depth - shift + count, count)
-        for t in range(2):
-            at = (owner * 2 + t) * deep
+def early_kernel(where_ref, alike_ref, table_ref, out_ref, all_ref):
+    parity, slot = where_ref[0], where_ref[1]
+    count, sides, _, deep, _ = alike_ref.shape
+    all_ref[...] = jnp.zeros_like(all_ref)
+    for k in range(count):
+        for t in range(sides):
+            at = ((2 * k + parity) * sides + t) * deep
             for p in range(4):
-                all_ref[p, pl.ds(pl.multiple_of(at, 8), deep), :] = piece[t, p]
+                all_ref[p, pl.ds(pl.multiple_of(at, 8), deep), :] = alike_ref[k, t, p]
     place, opposite_rows, opposite = table_ref[0], table_ref[1], table_ref[2]
 
     def placed(x):
@@ -274,6 +280,35 @@
     out_ref[0] = 0.5 * (placed(own) + reflected(jnp.where(packed, own, other)))
     out_ref[1] = 0.5 * (placed(jnp.where(packed, other, own)) + reflected(other))
     out_ref[2] = 0.5 * (placed(all_ref[2]) + reflected(all_ref[3]))
+
+
+def late_gains(where_ref, halves, early_ref, table_ref, rows_ref, late_ref):
+    parity, slot = where_ref[0], where_ref[1]
+    half, sides, _, deep, _ = halves[0].shape
+    size = sides * deep
+    for k in range(2 * half):
+        at = pl.multiple_of((2 * k + 1 - parity) * size, 16)
+        for i in range(2):
+            rows_ref[i, k * size : (k + 1) * size, :] = table_ref[i, pl.ds(at, size), :]
+        for t in range(sides):
+            for p in range(4):
+                late_ref[p, k * size + t * deep : k * size + (t + 1) * deep, :] = halves[k // half][k % half, t, p]
+    place, opposite_rows, opposite = rows_ref[0], rows_ref[1], table_ref[2]
+
+    def placed(x):
+        return sum(dot(place, piece, 0, 0) for piece in split2(x))
+
+    def reflected(x):
+        x = sum(dot(piece, opposite) for piece in split2(x))
+        return sum(dot(opposite_rows, piece, 0, 0) for piece in split2(x))
+
+    packed = slot == 0
+    own, other = late_ref[0], late_ref[1]
+    return (
+        early_ref[0] + 0.5 * (placed(own) + reflected(jnp.where(packed, own, other))),
+        early_ref[1] + 0.5 * (placed(jnp.where(packed, other, own)) + reflected(other)),
+        early_ref[2] + 0.5 * (placed(late_ref[2]) + reflected(late_ref[3])),
+    )
 
 
 def call(kernel, out_shape, operands, name, flops=0, scratch=(), spaces=None, out_space=pltpu.VMEM, vmem=VMEM_LIMIT):
@@ -292,7 +327,7 @@
 
 
 def spread(green):
-    depth_count = lax.axis_size("z")
+    depth_count = lax.axis_size("z") * lax.axis_size("parity")
     deep = green.shape[0]
     pick = jnp.asarray(pick_table().astype(ml_dtypes.bfloat16))
     sent = call(
@@ -309,29 +344,11 @@
     got = lax.all_to_all(sent, ("y_lo", "gy", "gz"), split_axis=0, concat_axis=0, tiled=True)
     pair = call(lay_kernel, (2, 4, deep, NG), (got.reshape(2 * 4 * GROUP, deep * 8),), "lay", flops=48 * 128 * 32 * 256)
     def along(value, by):
-        return lax.ppermute(value, "z", [(i, (i + by) % depth_count) for i in range(depth_count)])
-
-    from_ = {0: pair, 1: along(pair, 1), -1: along(pair, -1), 2: along(pair, 2), -2: along(pair, -2)}
-    from_[3] = along(from_[1], 2)
-    from_[-3] = along(from_[-1], -2)
-    from_[4] = along(from_[2], 2)
-    pieces = [from_[k] for k in (0, 1, 2, 3, 4, -3, -2, -1)]
-    return pieces
-
-
-def gains(pieces):
-    slot = lax.axis_index("gy") * GZ + lax.axis_index("gz")
-    where = jnp.stack([lax.axis_index("z"), slot]).astype(jnp.int32)
-    selections = jnp.asarray(gain_tables().astype(ml_dtypes.bfloat16))
-    return call(
-        gain_kernel,
-        (3, NG, NG),
-        (where, *pieces, selections),
-        "gain",
-        flops=54 * NG**3,
-        scratch=[pltpu.VMEM((4, NG, NG), F32)],
-        spaces=[pltpu.SMEM] + [pltpu.VMEM] * 9,
-    )
+        return lax.ppermute(value, ("z", "parity"), [(i, (i + by) % depth_count) for i in range(depth_count)])
+
+    alike = lax.all_gather(pair, "z")
+    half = alike.shape[0] // 2
+    return alike, along(alike[:half], 1), along(alike[half:], -1)
 
 
 def on_device(charges, green):
@@ -339,7 +356,7 @@
     there = [jnp.asarray(t) for t in parts_of(there)]
     back = [jnp.asarray(t) for t in parts_of(back)]
     tables = [jnp.asarray(t) for table in plane_tables() for t in parts_of(table)]
-    pieces = spread(green)
+    alike, *halves = spread(green)
     cells = ROWS * COLS
     chunks = HIGH // CHUNK
     sent = call(
@@ -362,13 +379,31 @@
         flops=6 * 16 * NG**3,
         scratch=[pltpu.VMEM((2 * NG, 2 * NG), F32)],
     )
-    spectra, *pieces[3:6] = lax.optimization_barrier((spectra, *pieces[3:6]))
+    slot = lax.axis_index("gy") * GZ + lax.axis_index("gz")
+    where = jnp.stack([lax.axis_index("parity"), slot]).astype(jnp.int32)
+    place, opposite_rows, opposite = gain_tables()
+    selections = jnp.asarray(np.stack([place, opposite_rows, opposite]).astype(ml_dtypes.bfloat16))
+    turned = jnp.asarray(np.stack([place.T, opposite_rows.T, opposite]).astype(ml_dtypes.bfloat16))
+    spectra, alike = lax.optimization_barrier((spectra, alike))
+    early = call(
+        early_kernel,
+        (3, NG, NG),
+        (where, alike, selections),
+        "early",
+        flops=36 * NG**3,
+        scratch=[pltpu.VMEM((4, NG, NG), F32)],
+        spaces=[pltpu.SMEM] + [pltpu.VMEM] * 2,
+    )
+    spectra, early, *halves = lax.optimization_barrier((spectra, early, *halves))
+    late_rows = NG // 2
     sent = call(
         back_kernel,
         (GROUP, ROWS, LANES),
-        (spectra, gains(pieces), *tables),
+        (where, spectra, early, *halves, turned, *tables),
         "back",
         flops=6 * 20 * NG**3,
+        spaces=[pltpu.SMEM] + [pltpu.VMEM] * 9,
+        scratch=[pltpu.VMEM((2, late_rows, NG), BF16), pltpu.VMEM((4, late_rows, NG), F32)],
     )
     got = lax.all_to_all(sent, ("gy", "gz"), split_axis=0, concat_axis=0, tiled=True)
     out = call(
@@ -384,13 +419,12 @@
 
 
 def solution(mesh):
-    apart = jax.sharding.Mesh(
-        mesh.devices.reshape(mesh.shape["rep"] // 2, 2, mesh.shape["gy"], mesh.shape["gz"]), ("z", "y_lo", "gy", "gz")
-    )
+    rep = ("z", "parity", "y_lo")
+    apart = jax.sharding.Mesh(mesh.devices.reshape(mesh.shape["rep"] // 4, 2, 2, GY, GZ), (*rep, "gy", "gz"))
     return jax.shard_map(
         on_device,
         mesh=apart,
-        in_specs=(P(("z", "y_lo", "gz"), "gy", None), P(("z", "y_lo"), ("gy", "gz"), None)),
-        out_specs=P(("z", "y_lo", "gz"), "gy", None),
+        in_specs=(P((*rep, "gz"), "gy", None), P(rep, ("gy", "gz"), None)),
+        out_specs=P((*rep, "gz"), "gy", None),
         check_vma=False,
     )

time: 110 us -> 109 us (level)
  blocking collectives: 38.3 us -> 61.1 us
  starting transfers between devices: 46 us -> 23.3 us
  waiting for transfers between devices: 10.2 us -> 7.25 us
    all_gather x0 -> x1, blocking collectives: none -> 22.8 us  [spread(): alike = lax.all_gather(pair, 'z')]
    ppermute x7 -> x2, starting transfers between devices: 29.6 us -> 7.04 us  [along(): lax.ppermute(value, ('z', 'parity'), [(i, (i + by) % depth_count) for i i...]
    ppermute x7 -> x2, waiting for transfers between devices: 4.93 us -> 2.03 us  [along(): lax.ppermute(value, ('z', 'parity'), [(i, (i + by) % depth_count) for i i...]
  transfers between devices with their start and end apart: 9 -> 4, of which waited for: 3 -> 2; matrix products, arithmetic and copies ran while one was open for 0% -> 1% of each run, Pallas kernels for 6% -> 8%
where the time goes in v2:
time: 109 us; the launch traced here: 108 us
  blocking collectives  61.1 us (56%)
  starting transfers between devices  23.3 us (21%)
  Pallas kernels  15.6 us (14%)
  waiting for transfers between devices  7.25 us (7%)
    all_to_all x1, blocking collectives, on_device(): lax.all_to_all(sent, ('gy', 'gz'), split_axis=0, concat_axis=0, tiled=True)  38.3 us
    all_gather x1, blocking collectives, spread(): alike = lax.all_gather(pair, 'z')  22.8 us
    pallas_call x7, Pallas kernels, call(): pl.pallas_call(kernel, out_shape=jax.ShapeDtypeStruct(out_shape, F32), in...  15.6 us
    all_to_all x1, starting transfers between devices, spread(): lax.all_to_all(sent, ('y_lo', 'gy', 'gz'), split_axis=0, concat_axis=0, t...  10.6 us
    ppermute x2, starting transfers between devices, along(): lax.ppermute(value, ('z', 'parity'), [(i, (i + by) % depth_count) for i i...  7.04 us
    all_to_all x1, starting transfers between devices, on_device(): lax.all_to_all(sent, ('gy', 'gz'), split_axis=0, concat_axis=0, tiled=True)  5.67 us
    all_to_all x1, waiting for transfers between devices, spread(): lax.all_to_all(sent, ('y_lo', 'gy', 'gz'), split_axis=0, concat_axis=0, t...  5.22 us
  transfers between devices with their start and end apart: 4, of which 2 were waited for; matrix products, arithmetic and copies ran while one was open for 1% of the time, Pallas kernels for 8%

profile of v2, /device:TPU:6, one launch (start us, length us, event | category | flops | bytes accessed | tf_op | source)
XLA Modules:
  0.0 108.4 jit_solution(6879498626876308757)
XLA Ops:
  0.0 1.7 %pick.1 = f32[256,128]{1,0:T(8,128)} custom-call(f32[128,128]{1,0:T(8,128)} %bitcast.18, bf16[128,128]{1,0:T(8,128)(2,1)} %constant.47.clone.pick_hbm), custom_call_target="tpu_custom_call" | custom-call | flops 12582912 | bytes 229376 | tf_op jit(solution)/shard_map/pick/pallas_call | solution.py:317
  1.7 10.6 %all-to-all-start.1 = ((f32[64,4,128]{2,1,0:T(4,128)}), f32[64,4,128]{2,1,0:T(4,128)S(1)}, u32[]{:S(2)}, u32[]{:S(2)}) async-start(f32[64,4,128]{2,1,0:T(4,128)} %bitcast.17), calls=%async_computation.1 | async-start | bytes 262144 | tf_op jit(solution)/shard_map/all_to_all | solution.py:344
  12.3 3.8 %depth.1 = f32[2048,128]{1,0:T(8,128)} custom-call(f32[2048,128]{1,0:T(8,128)} %bitcast.16, bf16[128,128]{1,0:T(8,128)(2,1)} %constant.39.clone.high_hbm, bf16[128,128]{1,0:T(8,128)(2,1)} %constant.40.clone.low_hbm), custom_call_target="tpu_custom_call" | custom-call | flops 201326592 | bytes 2162688 | tf_op jit(solution)/shard_map/depth/pallas_call | solution.py:317
  16.2 5.2 %all-to-all-done.1 = f32[64,4,128]{2,1,0:T(4,128)S(1)} async-done(((f32[64,4,128]{2,1,0:T(4,128)}), f32[64,4,128]{2,1,0:T(4,128)S(1)}, u32[]{:S(2)}, u32[]{:S(2)}) %all-to-all-start.1) | async-done | bytes 131104 | tf_op jit(solution)/shard_map/all_to_all | solution.py:344
  21.4 5.7 %all-to-all-start = ((f32[32,64,128]{2,1,0:T(8,128)}), f32[32,64,128]{2,1,0:T(8,128)S(1)}, u32[]{:S(2)}, u32[]{:S(2)}) async-start(f32[32,64,128]{2,1,0:T(8,128)} %bitcast.15), calls=%async_computation | async-start | bytes 2097152 | tf_op jit(solution)/shard_map/all_to_all | solution.py:373
  27.1 0.7 lay.1
  27.8 22.8 %all-gather = f32[8,4,16,256]{3,2,1,0:T(8,128)S(1)} all-gather(f32[2,4,16,256]{3,2,1,0:T(8,128)S(1)} %lay.1), channel_id=2, replica_groups=mesh['z'=4,'parity'=2,'y_lo'=2,'gy'=8,'gz'=4] {'z'}, dimensions={0}, use_global_device_ids=true | all-gather | bytes 655360 | tf_op jit(solution)/shard_map/all_gather | solution.py:349
  50.6 0.0 copy-start.4
  50.6 0.0 copy-start.5
  50.6 0.0 copy-start.6
  50.6 0.0 copy-start.7
  50.6 0.8 fusion
  51.5 3.4 %collective-permute-start = (f32[2,2,4,16,256]{4,3,2,1,0:T(8,128)}, f32[2,2,4,16,256]{4,3,2,1,0:T(8,128)S(1)}, u32[]{:S(2)}, u32[]{:S(2)}) collective-permute-start(f32[2,2,4,16,256]{4,3,2,1,0:T(8,128)} %bitcast.8), channel_id=1, source_target_pairs={{0,64},{64,128},{128,192},{192,256},{256,320},{320,384},{384,448},... | collective-permute-start | bytes 786440 | tf_op jit(solution)/shard_map/ppermute | solution.py:347
  54.9 3.6 %collective-permute-start.1 = (f32[2,2,4,16,256]{4,3,2,1,0:T(8,128)}, f32[2,2,4,16,256]{4,3,2,1,0:T(8,128)S(1)}, u32[]{:S(2)}, u32[]{:S(2)}) collective-permute-start(f32[2,2,4,16,256]{4,3,2,1,0:T(8,128)} %bitcast.9), channel_id=1, source_target_pairs={{0,448},{64,0},{128,64},{192,128},{256,192},{320,256},{384,320},{4... | collective-permute-start | bytes 786440 | tf_op jit(solution)/shard_map/ppermute | solution.py:347
  58.5 0.1 pad_add_fusion.where_ref
  58.6 0.0 copy-start.3
  58.6 0.0 all-to-all-done.r_ref
  58.6 0.0 copy-done.4
  58.6 0.0 copy-done.5
  58.6 0.0 copy-done.6
  58.6 0.0 copy-done.7
  58.6 2.3 %there.1.f_ref = f32[512,512]{1,0:T(8,128)S(1)} custom-call(f32[32,64,128]{2,1,0:T(8,128)S(1)} %all-to-all-done.r_ref, bf16[256,512]{1,0:T(8,128)(2,1)S(1)} %copy-done.7, bf16[256,512]{1,0:T(8,128)(2,1)S(1)} %copy-done.6, bf16[256,512]{1,0:T(8,128)(2,1)S(1)} %copy-done.5, bf16[256,512]{1,0:T(8,128)(2,1)S(1)} %copy-done.4), custom_call_target="tpu_custom_call" | custom-call | flops 1610612736 | bytes 3145728 | tf_op jit(solution)/shard_map/there/pallas_call | solution.py:317
  60.9 0.0 copy-done.3
  60.9 0.0 copy-start.2
  60.9 1.9 %early.1.early_ref = f32[3,256,256]{2,1,0:T(8,128)S(1)} custom-call(s32[2]{0:T(128)S(1)} %pad_add_fusion.where_ref, f32[4,2,4,16,256]{4,3,2,1,0:T(8,128)S(1)} %bitcast.13, bf16[3,256,256]{2,1,0:T(8,128)(2,1)S(1)} %copy-done.3), custom_call_target="tpu_custom_call" | custom-call | flops 603979776 | bytes 1703944 | tf_op jit(solution)/shard_map/early/pallas_call | solution.py:317
  62.8 0.0 collective-permute-done.refs_0_
  62.8 2.0 %collective-permute-done.1.refs_1_ = f32[2,2,4,16,256]{4,3,2,1,0:T(8,128)S(1)} collective-permute-done((f32[2,2,4,16,256]{4,3,2,1,0:T(8,128)}, f32[2,2,4,16,256]{4,3,2,1,0:T(8,128)S(1)}, u32[]{:S(2)}, u32[]{:S(2)}) %collective-permute-start.1) | collective-permute-done | bytes 262176 | tf_op jit(solution)/shard_map/ppermute | solution.py:347
  64.8 0.0 copy-done.2
  64.8 3.6 %back.1 = f32[32,64,128]{2,1,0:T(8,128)S(1)} custom-call(s32[2]{0:T(128)S(1)} %pad_add_fusion.where_ref, f32[512,512]{1,0:T(8,128)S(1)} %there.1.f_ref, f32[3,256,256]{2,1,0:T(8,128)S(1)} %early.1.early_ref, f32[2,2,4,16,256]{4,3,2,1,0:T(8,128)S(1)} %collective-permute-done.refs_0_, f32[2,2,4,16,256]{4,3,2,1,0:T(8,128)S(1)} %collective-permute-done.1.refs_1_, ...), custom_call_target="tpu_custom_call" | custom-call | flops 2013265920 | bytes 4849672 | tf_op jit(solution)/shard_map/back/pallas_call | solution.py:317
  68.5 0.0 copy-start
  68.5 0.0 copy-start.1
  68.5 38.3 %all_to_all.15 = f32[32,64,128]{2,1,0:T(8,128)S(1)} all-to-all(f32[32,64,128]{2,1,0:T(8,128)S(1)} %back.1), channel_id=1, replica_groups=mesh['z'=4,'parity'=2,'y_lo'=2,'gy'=8,'gz'=4] {'gy','gz'}, dimensions={0} | all-to-all | bytes 2097152 | tf_op jit(solution)/shard_map/all_to_all | solution.py:408
  106.8 0.0 copy-done
  106.8 0.0 copy-done.1
  106.8 1.6 %cells.1 = f32[2048,128]{1,0:T(8,128)} custom-call(f32[2048,128]{1,0:T(8,128)S(1)} %bitcast.12, bf16[128,128]{1,0:T(8,128)(2,1)S(1)} %copy-done.1, bf16[128,128]{1,0:T(8,128)(2,1)S(1)} %copy-done), custom_call_target="tpu_custom_call" | custom-call | flops 201326592 | bytes 2162688 | tf_op jit(solution)/shard_map/cells/pallas_call | solution.py:317
Async XLA Ops:
  1.7 19.7 %all-to-all-start.1 = ((f32[64,4,128]{2,1,0:T(4,128)}), f32[64,4,128]{2,1,0:T(4,128)S(1)}, u32[]{:S(2)}, u32[]{:S(2)}) async-start(f32[64,4,128]{2,1,0:T(4,128)} %bitcast.17), calls=%async_computation.1 | async-start | bytes 262144 | tf_op jit(solution)/shard_map/all_to_all | solution.py:344
  21.4 37.2 %all-to-all-start = ((f32[32,64,128]{2,1,0:T(8,128)}), f32[32,64,128]{2,1,0:T(8,128)S(1)}, u32[]{:S(2)}, u32[]{:S(2)}) async-start(f32[32,64,128]{2,1,0:T(8,128)} %bitcast.15), calls=%async_computation | async-start | bytes 2097152 | tf_op jit(solution)/shard_map/all_to_all | solution.py:373
  50.6 8.0 %copy-start.4 = (bf16[256,512]{1,0:T(8,128)(2,1)S(1)}, bf16[256,512]{1,0:T(8,128)(2,1)}, u32[]{:S(2)}) copy-start(bf16[256,512]{1,0:T(8,128)(2,1)} %constant.46.clone.rl.refs_6_) | copy-start | bytes 786436
  50.6 8.0 %copy-start.5 = (bf16[256,512]{1,0:T(8,128)(2,1)S(1)}, bf16[256,512]{1,0:T(8,128)(2,1)}, u32[]{:S(2)}) copy-start(bf16[256,512]{1,0:T(8,128)(2,1)} %constant.45.clone.rh.refs_5_) | copy-start | bytes 786436
  50.6 8.0 %copy-start.6 = (bf16[256,512]{1,0:T(8,128)(2,1)S(1)}, bf16[256,512]{1,0:T(8,128)(2,1)}, u32[]{:S(2)}) copy-start(bf16[256,512]{1,0:T(8,128)(2,1)} %constant.44.clone.ll.refs_4_) | copy-start | bytes 786436
  50.6 8.0 %copy-start.7 = (bf16[256,512]{1,0:T(8,128)(2,1)S(1)}, bf16[256,512]{1,0:T(8,128)(2,1)}, u32[]{:S(2)}) copy-start(bf16[256,512]{1,0:T(8,128)(2,1)} %constant.43.clone.lh.refs_3_) | copy-start | bytes 786436
  51.5 11.3 %collective-permute-start = (f32[2,2,4,16,256]{4,3,2,1,0:T(8,128)}, f32[2,2,4,16,256]{4,3,2,1,0:T(8,128)S(1)}, u32[]{:S(2)}, u32[]{:S(2)}) collective-permute-start(f32[2,2,4,16,256]{4,3,2,1,0:T(8,128)} %bitcast.8), channel_id=1, source_target_pairs={{0,64},{64,128},{128,192},{192,256},{256,320},{320,384},{384,448},... | collective-permute-start | bytes 786440 | tf_op jit(solution)/shard_map/ppermute | solution.py:347
  54.9 10.0 %collective-permute-start.1 = (f32[2,2,4,16,256]{4,3,2,1,0:T(8,128)}, f32[2,2,4,16,256]{4,3,2,1,0:T(8,128)S(1)}, u32[]{:S(2)}, u32[]{:S(2)}) collective-permute-start(f32[2,2,4,16,256]{4,3,2,1,0:T(8,128)} %bitcast.9), channel_id=1, source_target_pairs={{0,448},{64,0},{128,64},{192,128},{256,192},{320,256},{384,320},{4... | collective-permute-start | bytes 786440 | tf_op jit(solution)/shard_map/ppermute | solution.py:347
  58.6 2.3 %copy-start.3 = (bf16[3,256,256]{2,1,0:T(8,128)(2,1)S(1)}, bf16[3,256,256]{2,1,0:T(8,128)(2,1)}, u32[]{:S(2)}) copy-start(bf16[3,256,256]{2,1,0:T(8,128)(2,1)} %constant.48.clone.table_ref) | copy-start | bytes 1179652
  60.9 3.9 %copy-start.2 = (bf16[3,256,256]{2,1,0:T(8,128)(2,1)S(1)}, bf16[3,256,256]{2,1,0:T(8,128)(2,1)}, u32[]{:S(2)}) copy-start(bf16[3,256,256]{2,1,0:T(8,128)(2,1)} %constant.49.clone.refs_2_) | copy-start | bytes 1179652
  68.5 38.3 %copy-start = (bf16[128,128]{1,0:T(8,128)(2,1)S(1)}, bf16[128,128]{1,0:T(8,128)(2,1)}, u32[]{:S(2)}) copy-start(bf16[128,128]{1,0:T(8,128)(2,1)} %constant.42.clone.low_ref) | copy-start | bytes 98308
  68.5 38.3 %copy-start.1 = (bf16[128,128]{1,0:T(8,128)(2,1)S(1)}, bf16[128,128]{1,0:T(8,128)(2,1)}, u32[]{:S(2)}) copy-start(bf16[128,128]{1,0:T(8,128)(2,1)} %constant.41.clone.high_ref) | copy-start | bytes 98308

commit v3 on v2

--- a/solution.py
+++ b/solution.py
@@ -95,13 +95,6 @@
     return high, (x - high.astype(F32)).astype(BF16)
 
 
-def split3(x):
-    high = x.astype(BF16)
-    rest = x - high.astype(F32)
-    mid = rest.astype(BF16)
-    return high, mid, (rest - mid.astype(F32)).astype(BF16)
-
-
 def dot(a, b, da=1, db=0):
     return lax.dot_general(a, b, (((da,), (db,)), ((), ())), preferred_element_type=F32)
 
@@ -213,9 +206,10 @@
 
 
 def back_kernel(where_ref, f_ref, early_ref, *refs):
-    *halves, table_ref, lh, ll, rh, rl, out_ref, rows_ref, late_ref = refs
+    *parts, table_ref, lh, ll, rh, rl, out_ref, rows_ref, part_ref = refs
     columns = []
-    for p, gain in enumerate(late_gains(where_ref, halves, early_ref, table_ref, rows_ref, late_ref)):
+    for p, late in enumerate(share(parts, 1 - where_ref[0], where_ref[1], table_ref, rows_ref, part_ref)):
+        gain = early_ref[p] + late
         rows = slice(p // 2 * NG, (p // 2 + 1) * NG)
         columns.append(jnp.concatenate([f_ref[rows, :NG] * gain, f_ref[rows, NG:] * -gain], axis=0))
     u = dot(across(stacked(lh, ll, 1)), down(split2(jnp.concatenate(columns, axis=1))))
@@ -236,7 +230,7 @@
 def pick_kernel(g_hbm, pick_hbm, out_ref, g_ref, pick_ref, sems):
     wait(fetch((g_hbm, pick_hbm), (g_ref, pick_ref), sems))
     pick = pick_ref[...]
-    chosen = sum(dot(pick, piece, 1, 1) for piece in split3(g_ref[...]))
+    chosen = sum(dot(pick, piece, 1, 1) for piece in split2(g_ref[...]))
     for t in range(2):
         out_ref[t * 4 * GROUP : (t + 1) * 4 * GROUP, :] = chosen
 
@@ -252,47 +246,21 @@
     for t in range(2):
         for p in range(4):
             rows = g_ref[pl.ds(t * 4 * GROUP + p, GROUP, stride=4), :].T
-            wide = sum(dot(piece, grow) for piece in split3(rows))
+            wide = sum(dot(piece, grow) for piece in split2(rows))
             wide = jnp.where(keep, wide, 0.0)
             out_ref[t, p] = jnp.sum(wide.reshape(deep, 8, NG), axis=1)
 
 
-def early_kernel(where_ref, alike_ref, table_ref, out_ref, all_ref):
-    parity, slot = where_ref[0], where_ref[1]
-    count, sides, _, deep, _ = alike_ref.shape
-    all_ref[...] = jnp.zeros_like(all_ref)
-    for k in range(count):
-        for t in range(sides):
-            at = ((2 * k + parity) * sides + t) * deep
-            for p in range(4):
-                all_ref[p, pl.ds(pl.multiple_of(at, 8), deep), :] = alike_ref[k, t, p]
-    place, opposite_rows, opposite = table_ref[0], table_ref[1], table_ref[2]
-
-    def placed(x):
-        return sum(dot(place, piece) for piece in split2(x))
-
-    def reflected(x):
-        x = sum(dot(opposite_rows, piece) for piece in split2(x))
-        return sum(dot(piece, opposite) for piece in split2(x))
-
-    packed = slot == 0
-    own, other = all_ref[0], all_ref[1]
-    out_ref[0] = 0.5 * (placed(own) + reflected(jnp.where(packed, own, other)))
-    out_ref[1] = 0.5 * (placed(jnp.where(packed, other, own)) + reflected(other))
-    out_ref[2] = 0.5 * (placed(all_ref[2]) + reflected(all_ref[3]))
-
-
-def late_gains(where_ref, halves, early_ref, table_ref, rows_ref, late_ref):
-    parity, slot = where_ref[0], where_ref[1]
-    half, sides, _, deep, _ = halves[0].shape
-    size = sides * deep
-    for k in range(2 * half):
-        at = pl.multiple_of((2 * k + 1 - parity) * size, 16)
+def share(parts, other, slot, table_ref, rows_ref, part_ref):
+    deep = parts[0].shape[2]
+    blocks = [part.at[k] for part in parts for k in range(part.shape[0])]
+    for k, block in enumerate(blocks):
+        at = pl.multiple_of(((k // 2 * 2 + other) * 2 + k % 2) * deep, 16)
+        rows = slice(k * deep, (k + 1) * deep)
         for i in range(2):
-            rows_ref[i, k * size : (k + 1) * size, :] = table_ref[i, pl.ds(at, size), :]
-        for t in range(sides):
-            for p in range(4):
-                late_ref[p, k * size + t * deep : k * size + (t + 1) * deep, :] = halves[k // half][k % half, t, p]
+            rows_ref[i, rows, :] = table_ref[i, pl.ds(at, deep), :]
+        for p in range(4):
+            part_ref[p, rows, :] = block[p]
     place, opposite_rows, opposite = rows_ref[0], rows_ref[1], table_ref[2]
 
     def placed(x):
@@ -303,12 +271,17 @@
         return sum(dot(opposite_rows, piece, 0, 0) for piece in split2(x))
 
     packed = slot == 0
-    own, other = late_ref[0], late_ref[1]
+    own, far = part_ref[0], part_ref[1]
     return (
-        early_ref[0] + 0.5 * (placed(own) + reflected(jnp.where(packed, own, other))),
-        early_ref[1] + 0.5 * (placed(jnp.where(packed, other, own)) + reflected(other)),
-        early_ref[2] + 0.5 * (placed(late_ref[2]) + reflected(late_ref[3])),
-    )
+        0.5 * (placed(own) + reflected(jnp.where(packed, own, far))),
+        0.5 * (placed(jnp.where(packed, far, own)) + reflected(far)),
+        0.5 * (placed(part_ref[2]) + reflected(part_ref[3])),
+    )
+
+
+def early_kernel(where_ref, alike_ref, table_ref, out_ref, rows_ref, part_ref):
+    for p, gain in enumerate(share((alike_ref,), where_ref[0], where_ref[1], table_ref, rows_ref, part_ref)):
+        out_ref[p] = gain
 
 
 def call(kernel, out_shape, operands, name, flops=0, scratch=(), spaces=None, out_space=pltpu.VMEM, vmem=VMEM_LIMIT):
@@ -347,8 +320,9 @@
         return lax.ppermute(value, ("z", "parity"), [(i, (i + by) % depth_count) for i in range(depth_count)])
 
     alike = lax.all_gather(pair, "z")
-    half = alike.shape[0] // 2
-    return alike, along(alike[:half], 1), along(alike[half:], -1)
+    alike = alike.reshape(-1, *alike.shape[2:])
+    first = alike.shape[0] // 2 + 1
+    return alike, along(alike[:first], 1), along(alike[first:], -1)
 
 
 def on_device(charges, green):
@@ -356,7 +330,7 @@
     there = [jnp.asarray(t) for t in parts_of(there)]
     back = [jnp.asarray(t) for t in parts_of(back)]
     tables = [jnp.asarray(t) for table in plane_tables() for t in parts_of(table)]
-    alike, *halves = spread(green)
+    alike, *parts = spread(green)
     cells = ROWS * COLS
     chunks = HIGH // CHUNK
     sent = call(
@@ -382,28 +356,27 @@
     slot = lax.axis_index("gy") * GZ + lax.axis_index("gz")
     where = jnp.stack([lax.axis_index("parity"), slot]).astype(jnp.int32)
     place, opposite_rows, opposite = gain_tables()
-    selections = jnp.asarray(np.stack([place, opposite_rows, opposite]).astype(ml_dtypes.bfloat16))
     turned = jnp.asarray(np.stack([place.T, opposite_rows.T, opposite]).astype(ml_dtypes.bfloat16))
     spectra, alike = lax.optimization_barrier((spectra, alike))
+    share_scratch = [pltpu.VMEM((2, NG // 2, NG), BF16), pltpu.VMEM((4, NG // 2, NG), F32)]
     early = call(
         early_kernel,
         (3, NG, NG),
-        (where, alike, selections),
+        (where, alike, turned),
         "early",
-        flops=36 * NG**3,
-        scratch=[pltpu.VMEM((4, NG, NG), F32)],
+        flops=18 * NG**3,
+        scratch=share_scratch,
         spaces=[pltpu.SMEM] + [pltpu.VMEM] * 2,
     )
-    spectra, early, *halves = lax.optimization_barrier((spectra, early, *halves))
-    late_rows = NG // 2
+    spectra, early, *parts = lax.optimization_barrier((spectra, early, *parts))
     sent = call(
         back_kernel,
         (GROUP, ROWS, LANES),
-        (where, spectra, early, *halves, turned, *tables),
+        (where, spectra, early, *parts, turned, *tables),
         "back",
         flops=6 * 20 * NG**3,
         spaces=[pltpu.SMEM] + [pltpu.VMEM] * 9,
-        scratch=[pltpu.VMEM((2, late_rows, NG), BF16), pltpu.VMEM((4, late_rows, NG), F32)],
+        scratch=share_scratch,
     )
     got = lax.all_to_all(sent, ("gy", "gz"), split_axis=0, concat_axis=0, tiled=True)
     out = call(

time: 109 us -> 109 us (level)
  waiting for transfers between devices: 7.25 us -> 6.13 us
    ppermute x2, waiting for transfers between devices: 2.03 us -> 0.91 us  [along(): lax.ppermute(value, ('z', 'parity'), [(i, (i + by) % depth_count) for i i...]
where the time goes in v3:
time: 109 us; the launch traced here: 107 us
  blocking collectives  61 us (56%)
  starting transfers between devices  23.4 us (21%)
  Pallas kernels  15.2 us (14%)
  waiting for transfers between devices  6.13 us (6%)
  local copies, waits for them, and re-layouts  1.47 us (1%)
    all_to_all x1, blocking collectives, on_device(): lax.all_to_all(sent, ('gy', 'gz'), split_axis=0, concat_axis=0, tiled=True)  38.2 us
    all_gather x1, blocking collectives, spread(): alike = lax.all_gather(pair, 'z')  22.8 us
    pallas_call x7, Pallas kernels, call(): pl.pallas_call(kernel, out_shape=jax.ShapeDtypeStruct(out_shape, F32), in...  15.2 us
    all_to_all x1, starting transfers between devices, spread(): lax.all_to_all(sent, ('y_lo', 'gy', 'gz'), split_axis=0, concat_axis=0, t...  10.6 us
    ppermute x2, starting transfers between devices, along(): lax.ppermute(value, ('z', 'parity'), [(i, (i + by) % depth_count) for i i...  7.16 us
    all_to_all x1, starting transfers between devices, on_device(): lax.all_to_all(sent, ('gy', 'gz'), split_axis=0, concat_axis=0, tiled=True)  5.67 us
    all_to_all x1, waiting for transfers between devices, spread(): lax.all_to_all(sent, ('y_lo', 'gy', 'gz'), split_axis=0, concat_axis=0, t...  5.22 us
  transfers between devices with their start and end apart: 4, of which 2 were waited for; matrix products, arithmetic and copies ran while one was open for 1% of the time, Pallas kernels for 8%

profile of v3, /device:TPU:6, one launch (start us, length us, event | category | flops | bytes accessed | tf_op | source)
XLA Modules:
  0.0 107.5 jit_solution(16807157806617564066)
XLA Ops:
  0.0 1.7 %pick.1 = f32[256,128]{1,0:T(8,128)} custom-call(f32[128,128]{1,0:T(8,128)} %bitcast.14, bf16[128,128]{1,0:T(8,128)(2,1)} %constant.45.clone.pick_hbm), custom_call_target="tpu_custom_call" | custom-call | flops 12582912 | bytes 229376 | tf_op jit(solution)/shard_map/pick/pallas_call | solution.py:290
  1.7 10.6 %all-to-all-start.1 = ((f32[64,4,128]{2,1,0:T(4,128)}), f32[64,4,128]{2,1,0:T(4,128)S(1)}, u32[]{:S(2)}, u32[]{:S(2)}) async-start(f32[64,4,128]{2,1,0:T(4,128)} %bitcast.13), calls=%async_computation.1 | async-start | bytes 262144 | tf_op jit(solution)/shard_map/all_to_all | solution.py:317
  12.3 3.8 %depth.1 = f32[2048,128]{1,0:T(8,128)} custom-call(f32[2048,128]{1,0:T(8,128)} %bitcast.12, bf16[128,128]{1,0:T(8,128)(2,1)} %constant.37.clone.high_hbm, bf16[128,128]{1,0:T(8,128)(2,1)} %constant.38.clone.low_hbm), custom_call_target="tpu_custom_call" | custom-call | flops 201326592 | bytes 2162688 | tf_op jit(solution)/shard_map/depth/pallas_call | solution.py:290
  16.1 5.2 %all-to-all-done.1 = f32[64,4,128]{2,1,0:T(4,128)S(1)} async-done(((f32[64,4,128]{2,1,0:T(4,128)}), f32[64,4,128]{2,1,0:T(4,128)S(1)}, u32[]{:S(2)}, u32[]{:S(2)}) %all-to-all-start.1) | async-done | bytes 131104 | tf_op jit(solution)/shard_map/all_to_all | solution.py:317
  21.4 5.7 %all-to-all-start = ((f32[32,64,128]{2,1,0:T(8,128)}), f32[32,64,128]{2,1,0:T(8,128)S(1)}, u32[]{:S(2)}, u32[]{:S(2)}) async-start(f32[32,64,128]{2,1,0:T(8,128)} %bitcast.11), calls=%async_computation | async-start | bytes 2097152 | tf_op jit(solution)/shard_map/all_to_all | solution.py:347
  27.0 0.6 lay.1
  27.6 22.8 %all-gather.alike_ref = f32[8,4,16,256]{3,2,1,0:T(8,128)S(1)} all-gather(f32[2,4,16,256]{3,2,1,0:T(8,128)S(1)} %lay.1), channel_id=2, replica_groups=mesh['z'=4,'parity'=2,'y_lo'=2,'gy'=8,'gz'=4] {'z'}, dimensions={0}, use_global_device_ids=true | all-gather | bytes 655360 | tf_op jit(solution)/shard_map/all_gather | solution.py:322
  50.4 0.0 copy-start.4
  50.4 0.0 copy-start.5
  50.4 0.0 copy-start.6
  50.4 0.8 slice.8
  51.2 0.0 copy-start.3
  51.2 3.5 %collective-permute-start = (f32[5,4,16,256]{3,2,1,0:T(8,128)}, f32[5,4,16,256]{3,2,1,0:T(8,128)S(1)}, u32[]{:S(2)}, u32[]{:S(2)}) collective-permute-start(f32[5,4,16,256]{3,2,1,0:T(8,128)} %slice.8), channel_id=1, source_target_pairs={{0,64},{64,128},{128,192},{192,256},{256,320},{320,384},{384,448},... | collective-permute-start | bytes 983048 | tf_op jit(solution)/shard_map/ppermute | solution.py:320
  54.7 0.7 slice.9
  55.4 3.6 %collective-permute-start.1 = (f32[3,4,16,256]{3,2,1,0:T(8,128)}, f32[3,4,16,256]{3,2,1,0:T(8,128)S(1)}, u32[]{:S(2)}, u32[]{:S(2)}) collective-permute-start(f32[3,4,16,256]{3,2,1,0:T(8,128)} %slice.9), channel_id=1, source_target_pairs={{0,448},{64,0},{128,64},{192,128},{256,192},{320,256},{384,320},{4... | collective-permute-start | bytes 589832 | tf_op jit(solution)/shard_map/ppermute | solution.py:320
  59.0 0.1 pad_add_fusion.where_ref
  59.1 0.0 copy-start
  59.1 0.0 all-to-all-done.r_ref
  59.1 0.0 copy-done.4
  59.1 0.0 copy-done.5
  59.1 0.0 copy-done.6
  59.2 0.0 copy-done.3
  59.2 2.3 %there.1.f_ref = f32[512,512]{1,0:T(8,128)S(1)} custom-call(f32[32,64,128]{2,1,0:T(8,128)S(1)} %all-to-all-done.r_ref, bf16[256,512]{1,0:T(8,128)(2,1)S(1)} %copy-done.6, bf16[256,512]{1,0:T(8,128)(2,1)S(1)} %copy-done.5, bf16[256,512]{1,0:T(8,128)(2,1)S(1)} %copy-done.4, bf16[256,512]{1,0:T(8,128)(2,1)S(1)} %copy-done.3), custom_call_target="tpu_custom_call" | custom-call | flops 1610612736 | bytes 3145728 | tf_op jit(solution)/shard_map/there/pallas_call | solution.py:290
  61.4 0.0 copy-done
  61.4 1.6 %early.1.early_ref = f32[3,256,256]{2,1,0:T(8,128)S(1)} custom-call(s32[2]{0:T(128)S(1)} %pad_add_fusion.where_ref, f32[8,4,16,256]{3,2,1,0:T(8,128)S(1)} %all-gather.alike_ref, bf16[3,256,256]{2,1,0:T(8,128)(2,1)S(1)} %copy-done), custom_call_target="tpu_custom_call" | custom-call | flops 301989888 | bytes 1703944 | tf_op jit(solution)/shard_map/early/pallas_call | solution.py:290
  63.1 0.9 collective-permute-done.1.refs_1_
  64.0 0.0 collective-permute-done.refs_0_
  64.0 3.7 %back.1 = f32[32,64,128]{2,1,0:T(8,128)S(1)} custom-call(s32[2]{0:T(128)S(1)} %pad_add_fusion.where_ref, f32[512,512]{1,0:T(8,128)S(1)} %there.1.f_ref, f32[3,256,256]{2,1,0:T(8,128)S(1)} %early.1.early_ref, f32[5,4,16,256]{3,2,1,0:T(8,128)S(1)} %collective-permute-done.refs_0_, f32[3,4,16,256]{3,2,1,0:T(8,128)S(1)} %collective-permute-done.1.refs_1_, ...), custom_call_target="tpu_custom_call" | custom-call | flops 2013265920 | bytes 4849672 | tf_op jit(solution)/shard_map/back/pallas_call | solution.py:290
  67.6 0.0 copy-start.1
  67.6 0.0 copy-start.2
  67.6 38.2 %all_to_all.15 = f32[32,64,128]{2,1,0:T(8,128)S(1)} all-to-all(f32[32,64,128]{2,1,0:T(8,128)S(1)} %back.1), channel_id=1, replica_groups=mesh['z'=4,'parity'=2,'y_lo'=2,'gy'=8,'gz'=4] {'gy','gz'}, dimensions={0} | all-to-all | bytes 2097152 | tf_op jit(solution)/shard_map/all_to_all | solution.py:381
  105.9 0.0 copy-done.1
  105.9 0.0 copy-done.2
  105.9 1.6 %cells.1 = f32[2048,128]{1,0:T(8,128)} custom-call(f32[2048,128]{1,0:T(8,128)S(1)} %bitcast.9, bf16[128,128]{1,0:T(8,128)(2,1)S(1)} %copy-done.2, bf16[128,128]{1,0:T(8,128)(2,1)S(1)} %copy-done.1), custom_call_target="tpu_custom_call" | custom-call | flops 201326592 | bytes 2162688 | tf_op jit(solution)/shard_map/cells/pallas_call | solution.py:290
Async XLA Ops:
  1.7 19.7 %all-to-all-start.1 = ((f32[64,4,128]{2,1,0:T(4,128)}), f32[64,4,128]{2,1,0:T(4,128)S(1)}, u32[]{:S(2)}, u32[]{:S(2)}) async-start(f32[64,4,128]{2,1,0:T(4,128)} %bitcast.13), calls=%async_computation.1 | async-start | bytes 262144 | tf_op jit(solution)/shard_map/all_to_all | solution.py:317
  21.4 37.8 %all-to-all-start = ((f32[32,64,128]{2,1,0:T(8,128)}), f32[32,64,128]{2,1,0:T(8,128)S(1)}, u32[]{:S(2)}, u32[]{:S(2)}) async-start(f32[32,64,128]{2,1,0:T(8,128)} %bitcast.11), calls=%async_computation | async-start | bytes 2097152 | tf_op jit(solution)/shard_map/all_to_all | solution.py:347
  50.4 8.7 %copy-start.4 = (bf16[256,512]{1,0:T(8,128)(2,1)S(1)}, bf16[256,512]{1,0:T(8,128)(2,1)}, u32[]{:S(2)}) copy-start(bf16[256,512]{1,0:T(8,128)(2,1)} %constant.43.clone.rh.refs_5_) | copy-start | bytes 786436
  50.4 8.7 %copy-start.5 = (bf16[256,512]{1,0:T(8,128)(2,1)S(1)}, bf16[256,512]{1,0:T(8,128)(2,1)}, u32[]{:S(2)}) copy-start(bf16[256,512]{1,0:T(8,128)(2,1)} %constant.42.clone.ll.refs_4_) | copy-start | bytes 786436
  50.4 8.7 %copy-start.6 = (bf16[256,512]{1,0:T(8,128)(2,1)S(1)}, bf16[256,512]{1,0:T(8,128)(2,1)}, u32[]{:S(2)}) copy-start(bf16[256,512]{1,0:T(8,128)(2,1)} %constant.41.clone.lh.refs_3_) | copy-start | bytes 786436
  51.2 8.0 %copy-start.3 = (bf16[256,512]{1,0:T(8,128)(2,1)S(1)}, bf16[256,512]{1,0:T(8,128)(2,1)}, u32[]{:S(2)}) copy-start(bf16[256,512]{1,0:T(8,128)(2,1)} %constant.44.clone.rl.refs_6_) | copy-start | bytes 786436
  51.2 12.8 %collective-permute-start = (f32[5,4,16,256]{3,2,1,0:T(8,128)}, f32[5,4,16,256]{3,2,1,0:T(8,128)S(1)}, u32[]{:S(2)}, u32[]{:S(2)}) collective-permute-start(f32[5,4,16,256]{3,2,1,0:T(8,128)} %slice.8), channel_id=1, source_target_pairs={{0,64},{64,128},{128,192},{192,256},{256,320},{320,384},{384,448},... | collective-permute-start | bytes 983048 | tf_op jit(solution)/shard_map/ppermute | solution.py:320
  55.4 8.5 %collective-permute-start.1 = (f32[3,4,16,256]{3,2,1,0:T(8,128)}, f32[3,4,16,256]{3,2,1,0:T(8,128)S(1)}, u32[]{:S(2)}, u32[]{:S(2)}) collective-permute-start(f32[3,4,16,256]{3,2,1,0:T(8,128)} %slice.9), channel_id=1, source_target_pairs={{0,448},{64,0},{128,64},{192,128},{256,192},{320,256},{384,320},{4... | collective-permute-start | bytes 589832 | tf_op jit(solution)/shard_map/ppermute | solution.py:320
  59.1 2.3 %copy-start = (bf16[3,256,256]{2,1,0:T(8,128)(2,1)S(1)}, bf16[3,256,256]{2,1,0:T(8,128)(2,1)}, u32[]{:S(2)}) copy-start(bf16[3,256,256]{2,1,0:T(8,128)(2,1)} %constant.46.clone.table_ref.refs_2_) | copy-start | bytes 1179652
  67.6 38.3 %copy-start.1 = (bf16[128,128]{1,0:T(8,128)(2,1)S(1)}, bf16[128,128]{1,0:T(8,128)(2,1)}, u32[]{:S(2)}) copy-start(bf16[128,128]{1,0:T(8,128)(2,1)} %constant.40.clone.low_ref) | copy-start | bytes 98308
  67.6 38.3 %copy-start.2 = (bf16[128,128]{1,0:T(8,128)(2,1)S(1)}, bf16[128,128]{1,0:T(8,128)(2,1)}, u32[]{:S(2)}) copy-start(bf16[128,128]{1,0:T(8,128)(2,1)} %constant.39.clone.high_ref) | copy-start | bytes 98308

commit v4 on v3

--- a/solution.py
+++ b/solution.py
@@ -21,6 +21,7 @@
 LOW = LANES // COLS
 HIGH = ROWS // LOW
 CHUNK = 4
+OUT_CHUNK = 2
 
 VMEM_LIMIT = 16 * 1024 * 1024
 VMEM_ALL = 60 * 1024 * 1024
@@ -157,13 +158,13 @@
 
 def cells_kernel(r_ref, high_ref, low_ref, out_hbm, out_ref, sems):
     w = (high_ref[...], low_ref[...])
-    size = CHUNK * LANES
+    size = OUT_CHUNK * LANES
     copies = []
     for h in range(HIGH):
         t = jnp.concatenate([r_ref[pl.ds(c * HIGH + h, GROUP, stride=ROWS), :] for c in range(4)], axis=0)
-        out_ref[h * LANES : (h + 1) * LANES, :] = dot3(split2(t.T), w)
-        if h % CHUNK == CHUNK - 1:
-            i = h // CHUNK
+        out_ref[h * LANES : (h + 1) * LANES, :] = dot3(split2(t), w, 0, 0)
+        if h % OUT_CHUNK == OUT_CHUNK - 1:
+            i = h // OUT_CHUNK
             copies.append(
                 pltpu.make_async_copy(out_ref.at[i * size : (i + 1) * size], out_hbm.at[i * size : (i + 1) * size], sems.at[i])
             )
@@ -385,7 +386,7 @@
         (got.reshape(GROUP * ROWS, LANES), *back),
         "cells",
         flops=6 * cells * NZ * NZ,
-        scratch=[pltpu.VMEM((cells, NZ), F32), pltpu.SemaphoreType.DMA((chunks,))],
+        scratch=[pltpu.VMEM((cells, NZ), F32), pltpu.SemaphoreType.DMA((HIGH // OUT_CHUNK,))],
         out_space=pltpu.HBM,
     )
     return out.reshape(charges.shape)

time: 109 us -> 109 us (level)
  no operation moved by 1% of the time
where the time goes in v4:
time: 109 us; the launch traced here: 108 us
  blocking collectives  61 us (56%)
  starting transfers between devices  23.4 us (21%)
  Pallas kernels  15.3 us (14%)
  waiting for transfers between devices  6.13 us (6%)
  local copies, waits for them, and re-layouts  1.47 us (1%)
    all_to_all x1, blocking collectives, on_device(): lax.all_to_all(sent, ('gy', 'gz'), split_axis=0, concat_axis=0, tiled=True)  38.2 us
    all_gather x1, blocking collectives, spread(): alike = lax.all_gather(pair, 'z')  22.8 us
    pallas_call x7, Pallas kernels, call(): pl.pallas_call(kernel, out_shape=jax.ShapeDtypeStruct(out_shape, F32), in...  15.3 us
    all_to_all x1, starting transfers between devices, spread(): lax.all_to_all(sent, ('y_lo', 'gy', 'gz'), split_axis=0, concat_axis=0, t...  10.6 us
    ppermute x2, starting transfers between devices, along(): lax.ppermute(value, ('z', 'parity'), [(i, (i + by) % depth_count) for i i...  7.16 us
    all_to_all x1, starting transfers between devices, on_device(): lax.all_to_all(sent, ('gy', 'gz'), split_axis=0, concat_axis=0, tiled=True)  5.67 us
    all_to_all x1, waiting for transfers between devices, spread(): lax.all_to_all(sent, ('y_lo', 'gy', 'gz'), split_axis=0, concat_axis=0, t...  5.22 us
  transfers between devices with their start and end apart: 4, of which 2 were waited for; matrix products, arithmetic and copies ran while one was open for 1% of the time, Pallas kernels for 8%

profile of v4, /device:TPU:6, one launch (start us, length us, event | category | flops | bytes accessed | tf_op | source)
XLA Modules:
  0.0 107.5 jit_solution(2111916812327634594)
XLA Ops:
  0.0 1.7 %pick.1 = f32[256,128]{1,0:T(8,128)} custom-call(f32[128,128]{1,0:T(8,128)} %bitcast.14, bf16[128,128]{1,0:T(8,128)(2,1)} %constant.45.clone.pick_hbm), custom_call_target="tpu_custom_call" | custom-call | flops 12582912 | bytes 229376 | tf_op jit(solution)/shard_map/pick/pallas_call | solution.py:291
  1.7 10.6 %all-to-all-start.1 = ((f32[64,4,128]{2,1,0:T(4,128)}), f32[64,4,128]{2,1,0:T(4,128)S(1)}, u32[]{:S(2)}, u32[]{:S(2)}) async-start(f32[64,4,128]{2,1,0:T(4,128)} %bitcast.13), calls=%async_computation.1 | async-start | bytes 262144 | tf_op jit(solution)/shard_map/all_to_all | solution.py:318
  12.3 3.8 %depth.1 = f32[2048,128]{1,0:T(8,128)} custom-call(f32[2048,128]{1,0:T(8,128)} %bitcast.12, bf16[128,128]{1,0:T(8,128)(2,1)} %constant.37.clone.high_hbm, bf16[128,128]{1,0:T(8,128)(2,1)} %constant.38.clone.low_hbm), custom_call_target="tpu_custom_call" | custom-call | flops 201326592 | bytes 2162688 | tf_op jit(solution)/shard_map/depth/pallas_call | solution.py:291
  16.1 5.2 %all-to-all-done.1 = f32[64,4,128]{2,1,0:T(4,128)S(1)} async-done(((f32[64,4,128]{2,1,0:T(4,128)}), f32[64,4,128]{2,1,0:T(4,128)S(1)}, u32[]{:S(2)}, u32[]{:S(2)}) %all-to-all-start.1) | async-done | bytes 131104 | tf_op jit(solution)/shard_map/all_to_all | solution.py:318
  21.4 5.7 %all-to-all-start = ((f32[32,64,128]{2,1,0:T(8,128)}), f32[32,64,128]{2,1,0:T(8,128)S(1)}, u32[]{:S(2)}, u32[]{:S(2)}) async-start(f32[32,64,128]{2,1,0:T(8,128)} %bitcast.11), calls=%async_computation | async-start | bytes 2097152 | tf_op jit(solution)/shard_map/all_to_all | solution.py:348
  27.0 0.6 lay.1
  27.6 22.8 %all-gather.alike_ref = f32[8,4,16,256]{3,2,1,0:T(8,128)S(1)} all-gather(f32[2,4,16,256]{3,2,1,0:T(8,128)S(1)} %lay.1), channel_id=2, replica_groups=mesh['z'=4,'parity'=2,'y_lo'=2,'gy'=8,'gz'=4] {'z'}, dimensions={0}, use_global_device_ids=true | all-gather | bytes 655360 | tf_op jit(solution)/shard_map/all_gather | solution.py:323
  50.4 0.0 copy-start.4
  50.4 0.0 copy-start.5
  50.4 0.0 copy-start.6
  50.4 0.8 slice.8
  51.2 0.0 copy-start.3
  51.2 3.5 %collective-permute-start = (f32[5,4,16,256]{3,2,1,0:T(8,128)}, f32[5,4,16,256]{3,2,1,0:T(8,128)S(1)}, u32[]{:S(2)}, u32[]{:S(2)}) collective-permute-start(f32[5,4,16,256]{3,2,1,0:T(8,128)} %slice.8), channel_id=1, source_target_pairs={{0,64},{64,128},{128,192},{192,256},{256,320},{320,384},{384,448},... | collective-permute-start | bytes 983048 | tf_op jit(solution)/shard_map/ppermute | solution.py:321
  54.7 0.7 slice.9
  55.4 3.6 %collective-permute-start.1 = (f32[3,4,16,256]{3,2,1,0:T(8,128)}, f32[3,4,16,256]{3,2,1,0:T(8,128)S(1)}, u32[]{:S(2)}, u32[]{:S(2)}) collective-permute-start(f32[3,4,16,256]{3,2,1,0:T(8,128)} %slice.9), channel_id=1, source_target_pairs={{0,448},{64,0},{128,64},{192,128},{256,192},{320,256},{384,320},{4... | collective-permute-start | bytes 589832 | tf_op jit(solution)/shard_map/ppermute | solution.py:321
  59.0 0.1 pad_add_fusion.where_ref
  59.1 0.0 copy-start
  59.1 0.0 all-to-all-done.r_ref
  59.1 0.0 copy-done.4
  59.1 0.0 copy-done.5
  59.1 0.0 copy-done.6
  59.2 0.0 copy-done.3
  59.2 2.3 %there.1.f_ref = f32[512,512]{1,0:T(8,128)S(1)} custom-call(f32[32,64,128]{2,1,0:T(8,128)S(1)} %all-to-all-done.r_ref, bf16[256,512]{1,0:T(8,128)(2,1)S(1)} %copy-done.6, bf16[256,512]{1,0:T(8,128)(2,1)S(1)} %copy-done.5, bf16[256,512]{1,0:T(8,128)(2,1)S(1)} %copy-done.4, bf16[256,512]{1,0:T(8,128)(2,1)S(1)} %copy-done.3), custom_call_target="tpu_custom_call" | custom-call | flops 1610612736 | bytes 3145728 | tf_op jit(solution)/shard_map/there/pallas_call | solution.py:291
  61.4 0.0 copy-done
  61.4 1.6 %early.1.early_ref = f32[3,256,256]{2,1,0:T(8,128)S(1)} custom-call(s32[2]{0:T(128)S(1)} %pad_add_fusion.where_ref, f32[8,4,16,256]{3,2,1,0:T(8,128)S(1)} %all-gather.alike_ref, bf16[3,256,256]{2,1,0:T(8,128)(2,1)S(1)} %copy-done), custom_call_target="tpu_custom_call" | custom-call | flops 301989888 | bytes 1703944 | tf_op jit(solution)/shard_map/early/pallas_call | solution.py:291
  63.1 0.9 collective-permute-done.1.refs_1_
  64.0 0.0 collective-permute-done.refs_0_
  64.0 3.7 %back.1 = f32[32,64,128]{2,1,0:T(8,128)S(1)} custom-call(s32[2]{0:T(128)S(1)} %pad_add_fusion.where_ref, f32[512,512]{1,0:T(8,128)S(1)} %there.1.f_ref, f32[3,256,256]{2,1,0:T(8,128)S(1)} %early.1.early_ref, f32[5,4,16,256]{3,2,1,0:T(8,128)S(1)} %collective-permute-done.refs_0_, f32[3,4,16,256]{3,2,1,0:T(8,128)S(1)} %collective-permute-done.1.refs_1_, ...), custom_call_target="tpu_custom_call" | custom-call | flops 2013265920 | bytes 4849672 | tf_op jit(solution)/shard_map/back/pallas_call | solution.py:291
  67.6 0.0 copy-start.1
  67.6 0.0 copy-start.2
  67.6 38.2 %all_to_all.15 = f32[32,64,128]{2,1,0:T(8,128)S(1)} all-to-all(f32[32,64,128]{2,1,0:T(8,128)S(1)} %back.1), channel_id=1, replica_groups=mesh['z'=4,'parity'=2,'y_lo'=2,'gy'=8,'gz'=4] {'gy','gz'}, dimensions={0} | all-to-all | bytes 2097152 | tf_op jit(solution)/shard_map/all_to_all | solution.py:382
  105.9 0.0 copy-done.1
  105.9 0.0 copy-done.2
  105.9 1.6 %cells.1 = f32[2048,128]{1,0:T(8,128)} custom-call(f32[2048,128]{1,0:T(8,128)S(1)} %bitcast.9, bf16[128,128]{1,0:T(8,128)(2,1)S(1)} %copy-done.2, bf16[128,128]{1,0:T(8,128)(2,1)S(1)} %copy-done.1), custom_call_target="tpu_custom_call" | custom-call | flops 201326592 | bytes 2162688 | tf_op jit(solution)/shard_map/cells/pallas_call | solution.py:291
Async XLA Ops:
  1.7 19.7 %all-to-all-start.1 = ((f32[64,4,128]{2,1,0:T(4,128)}), f32[64,4,128]{2,1,0:T(4,128)S(1)}, u32[]{:S(2)}, u32[]{:S(2)}) async-start(f32[64,4,128]{2,1,0:T(4,128)} %bitcast.13), calls=%async_computation.1 | async-start | bytes 262144 | tf_op jit(solution)/shard_map/all_to_all | solution.py:318
  21.4 37.8 %all-to-all-start = ((f32[32,64,128]{2,1,0:T(8,128)}), f32[32,64,128]{2,1,0:T(8,128)S(1)}, u32[]{:S(2)}, u32[]{:S(2)}) async-start(f32[32,64,128]{2,1,0:T(8,128)} %bitcast.11), calls=%async_computation | async-start | bytes 2097152 | tf_op jit(solution)/shard_map/all_to_all | solution.py:348
  50.4 8.7 %copy-start.4 = (bf16[256,512]{1,0:T(8,128)(2,1)S(1)}, bf16[256,512]{1,0:T(8,128)(2,1)}, u32[]{:S(2)}) copy-start(bf16[256,512]{1,0:T(8,128)(2,1)} %constant.43.clone.rh.refs_5_) | copy-start | bytes 786436
  50.4 8.7 %copy-start.5 = (bf16[256,512]{1,0:T(8,128)(2,1)S(1)}, bf16[256,512]{1,0:T(8,128)(2,1)}, u32[]{:S(2)}) copy-start(bf16[256,512]{1,0:T(8,128)(2,1)} %constant.42.clone.ll.refs_4_) | copy-start | bytes 786436
  50.4 8.7 %copy-start.6 = (bf16[256,512]{1,0:T(8,128)(2,1)S(1)}, bf16[256,512]{1,0:T(8,128)(2,1)}, u32[]{:S(2)}) copy-start(bf16[256,512]{1,0:T(8,128)(2,1)} %constant.41.clone.lh.refs_3_) | copy-start | bytes 786436
  51.2 8.0 %copy-start.3 = (bf16[256,512]{1,0:T(8,128)(2,1)S(1)}, bf16[256,512]{1,0:T(8,128)(2,1)}, u32[]{:S(2)}) copy-start(bf16[256,512]{1,0:T(8,128)(2,1)} %constant.44.clone.rl.refs_6_) | copy-start | bytes 786436
  51.2 12.8 %collective-permute-start = (f32[5,4,16,256]{3,2,1,0:T(8,128)}, f32[5,4,16,256]{3,2,1,0:T(8,128)S(1)}, u32[]{:S(2)}, u32[]{:S(2)}) collective-permute-start(f32[5,4,16,256]{3,2,1,0:T(8,128)} %slice.8), channel_id=1, source_target_pairs={{0,64},{64,128},{128,192},{192,256},{256,320},{320,384},{384,448},... | collective-permute-start | bytes 983048 | tf_op jit(solution)/shard_map/ppermute | solution.py:321
  55.4 8.5 %collective-permute-start.1 = (f32[3,4,16,256]{3,2,1,0:T(8,128)}, f32[3,4,16,256]{3,2,1,0:T(8,128)S(1)}, u32[]{:S(2)}, u32[]{:S(2)}) collective-permute-start(f32[3,4,16,256]{3,2,1,0:T(8,128)} %slice.9), channel_id=1, source_target_pairs={{0,448},{64,0},{128,64},{192,128},{256,192},{320,256},{384,320},{4... | collective-permute-start | bytes 589832 | tf_op jit(solution)/shard_map/ppermute | solution.py:321
  59.1 2.3 %copy-start = (bf16[3,256,256]{2,1,0:T(8,128)(2,1)S(1)}, bf16[3,256,256]{2,1,0:T(8,128)(2,1)}, u32[]{:S(2)}) copy-start(bf16[3,256,256]{2,1,0:T(8,128)(2,1)} %constant.46.clone.table_ref.refs_2_) | copy-start | bytes 1179652
  67.6 38.3 %copy-start.1 = (bf16[128,128]{1,0:T(8,128)(2,1)S(1)}, bf16[128,128]{1,0:T(8,128)(2,1)}, u32[]{:S(2)}) copy-start(bf16[128,128]{1,0:T(8,128)(2,1)} %constant.40.clone.low_ref) | copy-start | bytes 98308
  67.6 38.3 %copy-start.2 = (bf16[128,128]{1,0:T(8,128)(2,1)S(1)}, bf16[128,128]{1,0:T(8,128)(2,1)}, u32[]{:S(2)}) copy-start(bf16[128,128]{1,0:T(8,128)(2,1)} %constant.39.clone.high_ref) | copy-start | bytes 98308

commit v5 on v1

--- a/solution.py
+++ b/solution.py
@@ -249,7 +249,8 @@
 
 
 def gain_kernel(where_ref, *refs):
-    *pieces, table_ref, out_ref, all_ref = refs
+    pair, low, high, far, below, above, table_ref, out_ref, all_ref = refs
+    pieces = [pair, below.at[0], low, below.at[1], far, above.at[1], high, above.at[0]]
     depth, slot = where_ref[0], where_ref[1]
     count = len(pieces)
     deep = NG // (2 * count)
@@ -311,11 +312,10 @@
     def along(value, by):
         return lax.ppermute(value, "z", [(i, (i + by) % depth_count) for i in range(depth_count)])
 
-    from_ = {0: pair, 1: along(pair, 1), -1: along(pair, -1), 2: along(pair, 2), -2: along(pair, -2)}
-    from_[3] = along(from_[1], 2)
-    from_[-3] = along(from_[-1], -2)
-    from_[4] = along(from_[2], 2)
-    pieces = [from_[k] for k in (0, 1, 2, 3, 4, -3, -2, -1)]
+    low, high = along(pair, 2), along(pair, -2)
+    opposite = along(low, 2)
+    below, above = along(jnp.stack([pair, low]), 1), along(jnp.stack([pair, high]), -1)
+    pieces = [pair, low, high, opposite, below, above]
     return pieces
 
 
@@ -330,7 +330,7 @@
         "gain",
         flops=54 * NG**3,
         scratch=[pltpu.VMEM((4, NG, NG), F32)],
-        spaces=[pltpu.SMEM] + [pltpu.VMEM] * 9,
+        spaces=[pltpu.SMEM] + [pltpu.VMEM] * 7,
     )
 
 
@@ -362,7 +362,7 @@
         flops=6 * 16 * NG**3,
         scratch=[pltpu.VMEM((2 * NG, 2 * NG), F32)],
     )
-    spectra, *pieces[3:6] = lax.optimization_barrier((spectra, *pieces[3:6]))
+    spectra, *pieces[3:] = lax.optimization_barrier((spectra, *pieces[3:]))
     sent = call(
         back_kernel,
         (GROUP, ROWS, LANES),

time: 110 us -> 111 us (level)
  starting transfers between devices: 46 us -> 41 us
  waiting for transfers between devices: 10.2 us -> 15.2 us
    ppermute x7 -> x5, waiting for transfers between devices: 4.93 us -> 9.99 us  [along(): lax.ppermute(value, 'z', [(i, (i + by) % depth_count) for i in range(dept...]
    ppermute x7 -> x5, starting transfers between devices: 29.6 us -> 24.7 us  [along(): lax.ppermute(value, 'z', [(i, (i + by) % depth_count) for i in range(dept...]
  transfers between devices with their start and end apart: 9 -> 7, of which waited for: 3 -> 4; matrix products, arithmetic and copies ran while one was open for 0% -> 1% of each run, Pallas kernels for 6% -> 6%
where the time goes in v5:
time: 111 us; the launch traced here: 110 us
  starting transfers between devices  41 us (37%)
  blocking collectives  38.3 us (35%)
  waiting for transfers between devices  15.2 us (14%)
  Pallas kernels  14.9 us (13%)
    all_to_all x1, blocking collectives, on_device(): lax.all_to_all(sent, ('gy', 'gz'), split_axis=0, concat_axis=0, tiled=True)  38.3 us
    ppermute x5, starting transfers between devices, along(): lax.ppermute(value, 'z', [(i, (i + by) % depth_count) for i in range(dept...  24.7 us
    pallas_call x7, Pallas kernels, call(): pl.pallas_call(kernel, out_shape=jax.ShapeDtypeStruct(out_shape, F32), in...  14.9 us
    all_to_all x1, starting transfers between devices, spread(): lax.all_to_all(sent, ('y_lo', 'gy', 'gz'), split_axis=0, concat_axis=0, t...  10.6 us
    ppermute x5, waiting for transfers between devices, along(): lax.ppermute(value, 'z', [(i, (i + by) % depth_count) for i in range(dept...  9.99 us
    all_to_all x1, starting transfers between devices, on_device(): lax.all_to_all(sent, ('gy', 'gz'), split_axis=0, concat_axis=0, tiled=True)  5.67 us
    all_to_all x1, waiting for transfers between devices, spread(): lax.all_to_all(sent, ('y_lo', 'gy', 'gz'), split_axis=0, concat_axis=0, t...  5.22 us
  transfers between devices with their start and end apart: 7, of which 4 were waited for; matrix products, arithmetic and copies ran while one was open for 1% of the time, Pallas kernels for 6%

profile of v5, /device:TPU:6, one launch (start us, length us, event | category | flops | bytes accessed | tf_op | source)
XLA Modules:
  0.0 110.5 jit_solution(1703674777399214762)
XLA Ops:
  0.0 1.7 %pick.1 = f32[256,128]{1,0:T(8,128)} custom-call(f32[128,128]{1,0:T(8,128)} %bitcast.20, bf16[128,128]{1,0:T(8,128)(2,1)} %constant.43.clone.pick_hbm), custom_call_target="tpu_custom_call" | custom-call | flops 12582912 | bytes 229376 | tf_op jit(solution)/shard_map/pick/pallas_call | solution.py:283
  1.7 10.6 %all-to-all-start.1 = ((f32[64,4,128]{2,1,0:T(4,128)}), f32[64,4,128]{2,1,0:T(4,128)S(1)}, u32[]{:S(2)}, u32[]{:S(2)}) async-start(f32[64,4,128]{2,1,0:T(4,128)} %bitcast.19), calls=%async_computation.1 | async-start | bytes 262144 | tf_op jit(solution)/shard_map/all_to_all | solution.py:310
  12.3 3.8 %depth.1 = f32[2048,128]{1,0:T(8,128)} custom-call(f32[2048,128]{1,0:T(8,128)} %bitcast.18, bf16[128,128]{1,0:T(8,128)(2,1)} %constant.35.clone.high_hbm, bf16[128,128]{1,0:T(8,128)(2,1)} %constant.36.clone.low_hbm), custom_call_target="tpu_custom_call" | custom-call | flops 201326592 | bytes 2162688 | tf_op jit(solution)/shard_map/depth/pallas_call | solution.py:283
  16.2 5.2 %all-to-all-done.1 = f32[64,4,128]{2,1,0:T(4,128)S(1)} async-done(((f32[64,4,128]{2,1,0:T(4,128)}), f32[64,4,128]{2,1,0:T(4,128)S(1)}, u32[]{:S(2)}, u32[]{:S(2)}) %all-to-all-start.1) | async-done | bytes 131104 | tf_op jit(solution)/shard_map/all_to_all | solution.py:310
  21.4 5.7 %all-to-all-start = ((f32[32,64,128]{2,1,0:T(8,128)}), f32[32,64,128]{2,1,0:T(8,128)S(1)}, u32[]{:S(2)}, u32[]{:S(2)}) async-start(f32[32,64,128]{2,1,0:T(8,128)} %bitcast.17), calls=%async_computation | async-start | bytes 2097152 | tf_op jit(solution)/shard_map/all_to_all | solution.py:356
  27.1 0.0 copy-start.6
  27.1 0.7 lay.1.refs_0_
  27.8 6.1 %collective-permute-start = (f32[2,4,16,256]{3,2,1,0:T(8,128)S(1)}, f32[2,4,16,256]{3,2,1,0:T(8,128)S(1)}, u32[]{:S(2)}, u32[]{:S(2)}) collective-permute-start(f32[2,4,16,256]{3,2,1,0:T(8,128)S(1)} %lay.1.refs_0_), channel_id=1, source_target_pairs={{0,128},{64,192},{128,256},{192,320},{256,384},{320,448},{384,0},{... | collective-permute-start | bytes 393224 | tf_op jit(solution)/shard_map/ppermute | solution.py:313
  33.9 6.8 %collective-permute-start.3 = (f32[2,4,16,256]{3,2,1,0:T(8,128)S(1)}, f32[2,4,16,256]{3,2,1,0:T(8,128)S(1)}, u32[]{:S(2)}, u32[]{:S(2)}) collective-permute-start(f32[2,4,16,256]{3,2,1,0:T(8,128)S(1)} %lay.1.refs_0_), channel_id=1, source_target_pairs={{0,384},{64,448},{128,0},{192,64},{256,128},{320,192},{384,256},{4... | collective-permute-start | bytes 393224 | tf_op jit(solution)/shard_map/ppermute | solution.py:313
  40.7 2.0 %collective-permute-done.refs_1_ = f32[2,4,16,256]{3,2,1,0:T(8,128)S(1)} collective-permute-done((f32[2,4,16,256]{3,2,1,0:T(8,128)S(1)}, f32[2,4,16,256]{3,2,1,0:T(8,128)S(1)}, u32[]{:S(2)}, u32[]{:S(2)}) %collective-permute-start) | collective-permute-done | bytes 131104 | tf_op jit(solution)/shard_map/ppermute | solution.py:313
  42.7 4.6 %collective-permute-done.3.refs_2_ = f32[2,4,16,256]{3,2,1,0:T(8,128)S(1)} collective-permute-done((f32[2,4,16,256]{3,2,1,0:T(8,128)S(1)}, f32[2,4,16,256]{3,2,1,0:T(8,128)S(1)}, u32[]{:S(2)}, u32[]{:S(2)}) %collective-permute-start.3) | collective-permute-done | bytes 131104 | tf_op jit(solution)/shard_map/ppermute | solution.py:313
  47.3 0.0 copy-start.3
  47.3 0.0 copy-start.4
  47.3 0.0 copy-start.5
  47.3 0.9 pad_maximum_fusion
  48.1 3.6 %collective-permute-start.2 = (f32[2,2,4,16,256]{4,3,2,1,0:T(8,128)}, f32[2,2,4,16,256]{4,3,2,1,0:T(8,128)S(1)}, u32[]{:S(2)}, u32[]{:S(2)}) collective-permute-start(f32[2,2,4,16,256]{4,3,2,1,0:T(8,128)} %get-tuple-element.14), channel_id=1, source_target_pairs={{0,64},{64,128},{128,192},{192,256},{256,320},{320,384},{384,448},... | collective-permute-start | bytes 786440 | tf_op jit(solution)/shard_map/ppermute | solution.py:313
  51.8 3.4 %collective-permute-start.4 = (f32[2,2,4,16,256]{4,3,2,1,0:T(8,128)}, f32[2,2,4,16,256]{4,3,2,1,0:T(8,128)S(1)}, u32[]{:S(2)}, u32[]{:S(2)}) collective-permute-start(f32[2,2,4,16,256]{4,3,2,1,0:T(8,128)} %get-tuple-element.13), channel_id=1, source_target_pairs={{0,448},{64,0},{128,64},{192,128},{256,192},{320,256},{384,320},{4... | collective-permute-start | bytes 786440 | tf_op jit(solution)/shard_map/ppermute | solution.py:313
  55.2 0.1 pad_add_fusion.where_ref
  55.3 0.0 copy-start.2
  55.3 4.8 %collective-permute-start.1 = (f32[2,4,16,256]{3,2,1,0:T(8,128)S(1)}, f32[2,4,16,256]{3,2,1,0:T(8,128)S(1)}, u32[]{:S(2)}, u32[]{:S(2)}) collective-permute-start(f32[2,4,16,256]{3,2,1,0:T(8,128)S(1)} %collective-permute-done.refs_1_), channel_id=1, source_target_pairs={{0,128},{64,192},{128,256},{192,320},{256,384},{320,448},{384,0},{... | collective-permute-start | bytes 393224 | tf_op jit(solution)/shard_map/ppermute | solution.py:313
  60.1 0.0 all-to-all-done.r_ref
  60.1 0.0 copy-done.6
  60.1 0.0 copy-done.3
  60.1 0.0 copy-done.4
  60.1 0.0 copy-done.5
  60.1 2.3 %there.1.f_ref = f32[512,512]{1,0:T(8,128)S(1)} custom-call(f32[32,64,128]{2,1,0:T(8,128)S(1)} %all-to-all-done.r_ref, bf16[256,512]{1,0:T(8,128)(2,1)S(1)} %copy-done.3, bf16[256,512]{1,0:T(8,128)(2,1)S(1)} %copy-done.4, bf16[256,512]{1,0:T(8,128)(2,1)S(1)} %copy-done.5, bf16[256,512]{1,0:T(8,128)(2,1)S(1)} %copy-done.6), custom_call_target="tpu_custom_call" | custom-call | flops 1610612736 | bytes 3145728 | tf_op jit(solution)/shard_map/there/pallas_call | solution.py:283
  62.4 3.4 %collective-permute-done.1.refs_3_ = f32[2,4,16,256]{3,2,1,0:T(8,128)S(1)} collective-permute-done((f32[2,4,16,256]{3,2,1,0:T(8,128)S(1)}, f32[2,4,16,256]{3,2,1,0:T(8,128)S(1)}, u32[]{:S(2)}, u32[]{:S(2)}) %collective-permute-start.1) | collective-permute-done | bytes 131104 | tf_op jit(solution)/shard_map/ppermute | solution.py:313
  65.8 0.0 collective-permute-done.2.refs_4_
  65.8 0.0 collective-permute-done.4.refs_5_
  65.8 0.0 copy-done.2
  65.8 1.8 %gain.1.gain_ref = f32[3,256,256]{2,1,0:T(8,128)S(1)} custom-call(s32[2]{0:T(128)S(1)} %pad_add_fusion.where_ref, f32[2,4,16,256]{3,2,1,0:T(8,128)S(1)} %lay.1.refs_0_, f32[2,4,16,256]{3,2,1,0:T(8,128)S(1)} %collective-permute-done.refs_1_, f32[2,4,16,256]{3,2,1,0:T(8,128)S(1)} %collective-permute-done.3.refs_2_, ...), custom_call_target="tpu_custom_call" | custom-call | flops 905969664 | bytes 2228232 | tf_op jit(solution)/shard_map/gain/pallas_call | solution.py:283
  67.7 2.9 %back.1 = f32[32,64,128]{2,1,0:T(8,128)S(1)} custom-call(f32[512,512]{1,0:T(8,128)S(1)} %there.1.f_ref, f32[3,256,256]{2,1,0:T(8,128)S(1)} %gain.1.gain_ref, bf16[256,512]{1,0:T(8,128)(2,1)S(1)} %copy-done.3, bf16[256,512]{1,0:T(8,128)(2,1)S(1)} %copy-done.4, bf16[256,512]{1,0:T(8,128)(2,1)S(1)} %copy-done.5, bf16[256,512]{1,0:T(8,128)(2,1)S(1)} %copy-done.6), custom_call_target="tpu_custom_call" | custom-call | flops 2013265920 | bytes 3932160 | tf_op jit(solution)/shard_map/back/pallas_call | solution.py:283
  70.6 0.0 copy-start
  70.6 0.0 copy-start.1
  70.6 38.3 %all_to_all.15 = f32[32,64,128]{2,1,0:T(8,128)S(1)} all-to-all(f32[32,64,128]{2,1,0:T(8,128)S(1)} %back.1), channel_id=1, replica_groups=mesh['z'=8,'y_lo'=2,'gy'=8,'gz'=4] {'gy','gz'}, dimensions={0} | all-to-all | bytes 2097152 | tf_op jit(solution)/shard_map/all_to_all | solution.py:373
  108.9 0.0 copy-done
  108.9 0.0 copy-done.1
  108.9 1.6 %cells.1 = f32[2048,128]{1,0:T(8,128)} custom-call(f32[2048,128]{1,0:T(8,128)S(1)} %bitcast.12, bf16[128,128]{1,0:T(8,128)(2,1)S(1)} %copy-done, bf16[128,128]{1,0:T(8,128)(2,1)S(1)} %copy-done.1), custom_call_target="tpu_custom_call" | custom-call | flops 201326592 | bytes 2162688 | tf_op jit(solution)/shard_map/cells/pallas_call | solution.py:283
Async XLA Ops:
  1.7 19.7 %all-to-all-start.1 = ((f32[64,4,128]{2,1,0:T(4,128)}), f32[64,4,128]{2,1,0:T(4,128)S(1)}, u32[]{:S(2)}, u32[]{:S(2)}) async-start(f32[64,4,128]{2,1,0:T(4,128)} %bitcast.19), calls=%async_computation.1 | async-start | bytes 262144 | tf_op jit(solution)/shard_map/all_to_all | solution.py:310
  21.4 38.7 %all-to-all-start = ((f32[32,64,128]{2,1,0:T(8,128)}), f32[32,64,128]{2,1,0:T(8,128)S(1)}, u32[]{:S(2)}, u32[]{:S(2)}) async-start(f32[32,64,128]{2,1,0:T(8,128)} %bitcast.17), calls=%async_computation | async-start | bytes 2097152 | tf_op jit(solution)/shard_map/all_to_all | solution.py:356
  27.1 33.0 %copy-start.6 = (bf16[256,512]{1,0:T(8,128)(2,1)S(1)}, bf16[256,512]{1,0:T(8,128)(2,1)}, u32[]{:S(2)}) copy-start(bf16[256,512]{1,0:T(8,128)(2,1)} %constant.42.clone.rl) | copy-start | bytes 786436
  27.8 14.9 %collective-permute-start = (f32[2,4,16,256]{3,2,1,0:T(8,128)S(1)}, f32[2,4,16,256]{3,2,1,0:T(8,128)S(1)}, u32[]{:S(2)}, u32[]{:S(2)}) collective-permute-start(f32[2,4,16,256]{3,2,1,0:T(8,128)S(1)} %lay.1.refs_0_), channel_id=1, source_target_pairs={{0,128},{64,192},{128,256},{192,320},{256,384},{320,448},{384,0},{... | collective-permute-start | bytes 393224 | tf_op jit(solution)/shard_map/ppermute | solution.py:313
  33.9 13.4 %collective-permute-start.3 = (f32[2,4,16,256]{3,2,1,0:T(8,128)S(1)}, f32[2,4,16,256]{3,2,1,0:T(8,128)S(1)}, u32[]{:S(2)}, u32[]{:S(2)}) collective-permute-start(f32[2,4,16,256]{3,2,1,0:T(8,128)S(1)} %lay.1.refs_0_), channel_id=1, source_target_pairs={{0,384},{64,448},{128,0},{192,64},{256,128},{320,192},{384,256},{4... | collective-permute-start | bytes 393224 | tf_op jit(solution)/shard_map/ppermute | solution.py:313
  47.3 12.8 %copy-start.3 = (bf16[256,512]{1,0:T(8,128)(2,1)S(1)}, bf16[256,512]{1,0:T(8,128)(2,1)}, u32[]{:S(2)}) copy-start(bf16[256,512]{1,0:T(8,128)(2,1)} %constant.39.clone.lh) | copy-start | bytes 786436
  47.3 12.8 %copy-start.4 = (bf16[256,512]{1,0:T(8,128)(2,1)S(1)}, bf16[256,512]{1,0:T(8,128)(2,1)}, u32[]{:S(2)}) copy-start(bf16[256,512]{1,0:T(8,128)(2,1)} %constant.40.clone.ll) | copy-start | bytes 786436
  47.3 12.8 %copy-start.5 = (bf16[256,512]{1,0:T(8,128)(2,1)S(1)}, bf16[256,512]{1,0:T(8,128)(2,1)}, u32[]{:S(2)}) copy-start(bf16[256,512]{1,0:T(8,128)(2,1)} %constant.41.clone.rh) | copy-start | bytes 786436
  48.1 17.7 %collective-permute-start.2 = (f32[2,2,4,16,256]{4,3,2,1,0:T(8,128)}, f32[2,2,4,16,256]{4,3,2,1,0:T(8,128)S(1)}, u32[]{:S(2)}, u32[]{:S(2)}) collective-permute-start(f32[2,2,4,16,256]{4,3,2,1,0:T(8,128)} %get-tuple-element.14), channel_id=1, source_target_pairs={{0,64},{64,128},{128,192},{192,256},{256,320},{320,384},{384,448},... | collective-permute-start | bytes 786440 | tf_op jit(solution)/shard_map/ppermute | solution.py:313
  51.8 14.1 %collective-permute-start.4 = (f32[2,2,4,16,256]{4,3,2,1,0:T(8,128)}, f32[2,2,4,16,256]{4,3,2,1,0:T(8,128)S(1)}, u32[]{:S(2)}, u32[]{:S(2)}) collective-permute-start(f32[2,2,4,16,256]{4,3,2,1,0:T(8,128)} %get-tuple-element.13), channel_id=1, source_target_pairs={{0,448},{64,0},{128,64},{192,128},{256,192},{320,256},{384,320},{4... | collective-permute-start | bytes 786440 | tf_op jit(solution)/shard_map/ppermute | solution.py:313
  55.3 10.5 %copy-start.2 = (bf16[3,256,256]{2,1,0:T(8,128)(2,1)S(1)}, bf16[3,256,256]{2,1,0:T(8,128)(2,1)}, u32[]{:S(2)}) copy-start(bf16[3,256,256]{2,1,0:T(8,128)(2,1)} %constant.44.clone.refs_6_) | copy-start | bytes 1179652
  55.3 10.5 %collective-permute-start.1 = (f32[2,4,16,256]{3,2,1,0:T(8,128)S(1)}, f32[2,4,16,256]{3,2,1,0:T(8,128)S(1)}, u32[]{:S(2)}, u32[]{:S(2)}) collective-permute-start(f32[2,4,16,256]{3,2,1,0:T(8,128)S(1)} %collective-permute-done.refs_1_), channel_id=1, source_target_pairs={{0,128},{64,192},{128,256},{192,320},{256,384},{320,448},{384,0},{... | collective-permute-start | bytes 393224 | tf_op jit(solution)/shard_map/ppermute | solution.py:313
  70.6 38.3 %copy-start = (bf16[128,128]{1,0:T(8,128)(2,1)S(1)}, bf16[128,128]{1,0:T(8,128)(2,1)}, u32[]{:S(2)}) copy-start(bf16[128,128]{1,0:T(8,128)(2,1)} %constant.37.clone.high_ref) | copy-start | bytes 98308
  70.6 38.3 %copy-start.1 = (bf16[128,128]{1,0:T(8,128)(2,1)S(1)}, bf16[128,128]{1,0:T(8,128)(2,1)}, u32[]{:S(2)}) copy-start(bf16[128,128]{1,0:T(8,128)(2,1)} %constant.38.clone.low_ref) | copy-start | bytes 98308

commit v6 on v2

--- a/solution.py
+++ b/solution.py
@@ -213,9 +213,9 @@
 
 
 def back_kernel(where_ref, f_ref, early_ref, *refs):
-    *halves, table_ref, lh, ll, rh, rl, out_ref, rows_ref, late_ref = refs
+    *parts, table_ref, lh, ll, rh, rl, out_ref, rows_ref, late_ref = refs
     columns = []
-    for p, gain in enumerate(late_gains(where_ref, halves, early_ref, table_ref, rows_ref, late_ref)):
+    for p, gain in enumerate(late_gains(where_ref, parts, early_ref, table_ref, rows_ref, late_ref)):
         rows = slice(p // 2 * NG, (p // 2 + 1) * NG)
         columns.append(jnp.concatenate([f_ref[rows, :NG] * gain, f_ref[rows, NG:] * -gain], axis=0))
     u = dot(across(stacked(lh, ll, 1)), down(split2(jnp.concatenate(columns, axis=1))))
@@ -259,13 +259,12 @@
 
 def early_kernel(where_ref, alike_ref, table_ref, out_ref, all_ref):
     parity, slot = where_ref[0], where_ref[1]
-    count, sides, _, deep, _ = alike_ref.shape
+    count, _, deep, _ = alike_ref.shape
     all_ref[...] = jnp.zeros_like(all_ref)
     for k in range(count):
-        for t in range(sides):
-            at = ((2 * k + parity) * sides + t) * deep
-            for p in range(4):
-                all_ref[p, pl.ds(pl.multiple_of(at, 8), deep), :] = alike_ref[k, t, p]
+        at = ((k // 2 * 2 + parity) * 2 + k % 2) * deep
+        for p in range(4):
+            all_ref[p, pl.ds(pl.multiple_of(at, 8), deep), :] = alike_ref[k, p]
     place, opposite_rows, opposite = table_ref[0], table_ref[1], table_ref[2]
 
     def placed(x):
@@ -282,17 +281,17 @@
     out_ref[2] = 0.5 * (placed(all_ref[2]) + reflected(all_ref[3]))
 
 
-def late_gains(where_ref, halves, early_ref, table_ref, rows_ref, late_ref):
+def late_gains(where_ref, parts, early_ref, table_ref, rows_ref, late_ref):
     parity, slot = where_ref[0], where_ref[1]
-    half, sides, _, deep, _ = halves[0].shape
-    size = sides * deep
-    for k in range(2 * half):
-        at = pl.multiple_of((2 * k + 1 - parity) * size, 16)
+    first, _, deep, _ = parts[0].shape
+    for k in range(first + parts[1].shape[0]):
+        at = pl.multiple_of(((k // 2 * 2 + 1 - parity) * 2 + k % 2) * deep, 16)
+        rows = slice(k * deep, (k + 1) * deep)
         for i in range(2):
-            rows_ref[i, k * size : (k + 1) * size, :] = table_ref[i, pl.ds(at, size), :]
-        for t in range(sides):
-            for p in range(4):
-                late_ref[p, k * size + t * deep : k * size + (t + 1) * deep, :] = halves[k // half][k % half, t, p]
+            rows_ref[i, rows, :] = table_ref[i, pl.ds(at, deep), :]
+        part, n = (parts[0], k) if k < first else (parts[1], k - first)
+        for p in range(4):
+            late_ref[p, rows, :] = part[n, p]
     place, opposite_rows, opposite = rows_ref[0], rows_ref[1], table_ref[2]
 
     def placed(x):
@@ -347,8 +346,9 @@
         return lax.ppermute(value, ("z", "parity"), [(i, (i + by) % depth_count) for i in range(depth_count)])
 
     alike = lax.all_gather(pair, "z")
-    half = alike.shape[0] // 2
-    return alike, along(alike[:half], 1), along(alike[half:], -1)
+    alike = alike.reshape(-1, *alike.shape[2:])
+    first = alike.shape[0] // 2 + 1
+    return alike, along(alike[:first], 1), along(alike[first:], -1)
 
 
 def on_device(charges, green):
@@ -356,7 +356,7 @@
     there = [jnp.asarray(t) for t in parts_of(there)]
     back = [jnp.asarray(t) for t in parts_of(back)]
     tables = [jnp.asarray(t) for table in plane_tables() for t in parts_of(table)]
-    alike, *halves = spread(green)
+    alike, *parts = spread(green)
     cells = ROWS * COLS
     chunks = HIGH // CHUNK
     sent = call(
@@ -394,12 +394,12 @@
         scratch=[pltpu.VMEM((4, NG, NG), F32)],
         spaces=[pltpu.SMEM] + [pltpu.VMEM] * 2,
     )
-    spectra, early, *halves = lax.optimization_barrier((spectra, early, *halves))
+    spectra, early, *parts = lax.optimization_barrier((spectra, early, *parts))
     late_rows = NG // 2
     sent = call(
         back_kernel,
         (GROUP, ROWS, LANES),
-        (where, spectra, early, *halves, turned, *tables),
+        (where, spectra, early, *parts, turned, *tables),
         "back",
         flops=6 * 20 * NG**3,
         spaces=[pltpu.SMEM] + [pltpu.VMEM] * 9,

time: 109 us -> 108 us (level)
  waiting for transfers between devices: 7.25 us -> 5.91 us
    ppermute x2, waiting for transfers between devices: 2.03 us -> 0.69 us  [along(): lax.ppermute(value, ('z', 'parity'), [(i, (i + by) % depth_count) for i i...]
where the time goes in v6:
time: 108 us
  blocking collectives  61 us (56%)
  starting transfers between devices  23.6 us (22%)
  Pallas kernels  15.6 us (14%)
  waiting for transfers between devices  5.91 us (5%)
  local copies, waits for them, and re-layouts  1.46 us (1%)
    all_to_all x1, blocking collectives, on_device(): lax.all_to_all(sent, ('gy', 'gz'), split_axis=0, concat_axis=0, tiled=True)  38.2 us
    all_gather x1, blocking collectives, spread(): alike = lax.all_gather(pair, 'z')  22.8 us
    pallas_call x7, Pallas kernels, call(): pl.pallas_call(kernel, out_shape=jax.ShapeDtypeStruct(out_shape, F32), in...  15.6 us
    all_to_all x1, starting transfers between devices, spread(): lax.all_to_all(sent, ('y_lo', 'gy', 'gz'), split_axis=0, concat_axis=0, t...  10.6 us
    ppermute x2, starting transfers between devices, along(): lax.ppermute(value, ('z', 'parity'), [(i, (i + by) % depth_count) for i i...  7.29 us
    all_to_all x1, starting transfers between devices, on_device(): lax.all_to_all(sent, ('gy', 'gz'), split_axis=0, concat_axis=0, tiled=True)  5.67 us
    all_to_all x1, waiting for transfers between devices, spread(): lax.all_to_all(sent, ('y_lo', 'gy', 'gz'), split_axis=0, concat_axis=0, t...  5.22 us
  transfers between devices with their start and end apart: 4, of which 2 were waited for; matrix products, arithmetic and copies ran while one was open for 1% of the time, Pallas kernels for 8%

profile of v6, /device:TPU:6, one launch (start us, length us, event | category | flops | bytes accessed | tf_op | source)
XLA Modules:
  0.0 107.8 jit_solution(5021308011178518110)
XLA Ops:
  0.0 1.7 %pick.1 = f32[256,128]{1,0:T(8,128)} custom-call(f32[128,128]{1,0:T(8,128)} %bitcast.14, bf16[128,128]{1,0:T(8,128)(2,1)} %constant.47.clone.pick_hbm), custom_call_target="tpu_custom_call" | custom-call | flops 12582912 | bytes 229376 | tf_op jit(solution)/shard_map/pick/pallas_call | solution.py:316
  1.7 10.6 %all-to-all-start.1 = ((f32[64,4,128]{2,1,0:T(4,128)}), f32[64,4,128]{2,1,0:T(4,128)S(1)}, u32[]{:S(2)}, u32[]{:S(2)}) async-start(f32[64,4,128]{2,1,0:T(4,128)} %bitcast.13), calls=%async_computation.1 | async-start | bytes 262144 | tf_op jit(solution)/shard_map/all_to_all | solution.py:343
  12.3 3.8 %depth.1 = f32[2048,128]{1,0:T(8,128)} custom-call(f32[2048,128]{1,0:T(8,128)} %bitcast.12, bf16[128,128]{1,0:T(8,128)(2,1)} %constant.39.clone.high_hbm, bf16[128,128]{1,0:T(8,128)(2,1)} %constant.40.clone.low_hbm), custom_call_target="tpu_custom_call" | custom-call | flops 201326592 | bytes 2162688 | tf_op jit(solution)/shard_map/depth/pallas_call | solution.py:316
  16.2 5.2 %all-to-all-done.1 = f32[64,4,128]{2,1,0:T(4,128)S(1)} async-done(((f32[64,4,128]{2,1,0:T(4,128)}), f32[64,4,128]{2,1,0:T(4,128)S(1)}, u32[]{:S(2)}, u32[]{:S(2)}) %all-to-all-start.1) | async-done | bytes 131104 | tf_op jit(solution)/shard_map/all_to_all | solution.py:343
  21.4 5.7 %all-to-all-start = ((f32[32,64,128]{2,1,0:T(8,128)}), f32[32,64,128]{2,1,0:T(8,128)S(1)}, u32[]{:S(2)}, u32[]{:S(2)}) async-start(f32[32,64,128]{2,1,0:T(8,128)} %bitcast.11), calls=%async_computation | async-start | bytes 2097152 | tf_op jit(solution)/shard_map/all_to_all | solution.py:373
  27.1 0.7 lay.1
  27.8 22.8 %all-gather.alike_ref = f32[8,4,16,256]{3,2,1,0:T(8,128)S(1)} all-gather(f32[2,4,16,256]{3,2,1,0:T(8,128)S(1)} %lay.1), channel_id=2, replica_groups=mesh['z'=4,'parity'=2,'y_lo'=2,'gy'=8,'gz'=4] {'z'}, dimensions={0}, use_global_device_ids=true | all-gather | bytes 655360 | tf_op jit(solution)/shard_map/all_gather | solution.py:348
  50.6 0.0 copy-start.5
  50.6 0.0 copy-start.6
  50.6 0.0 copy-start.7
  50.6 0.7 slice.8
  51.3 0.0 copy-start.4
  51.3 3.5 %collective-permute-start = (f32[5,4,16,256]{3,2,1,0:T(8,128)}, f32[5,4,16,256]{3,2,1,0:T(8,128)S(1)}, u32[]{:S(2)}, u32[]{:S(2)}) collective-permute-start(f32[5,4,16,256]{3,2,1,0:T(8,128)} %slice.8), channel_id=1, source_target_pairs={{0,64},{64,128},{128,192},{192,256},{256,320},{320,384},{384,448},... | collective-permute-start | bytes 983048 | tf_op jit(solution)/shard_map/ppermute | solution.py:346
  54.9 0.1 pad_add_fusion.where_ref
  55.0 0.7 slice.9
  55.6 0.0 copy-start.3
  55.6 3.8 %collective-permute-start.1 = (f32[3,4,16,256]{3,2,1,0:T(8,128)}, f32[3,4,16,256]{3,2,1,0:T(8,128)S(1)}, u32[]{:S(2)}, u32[]{:S(2)}) collective-permute-start(f32[3,4,16,256]{3,2,1,0:T(8,128)} %slice.9), channel_id=1, source_target_pairs={{0,448},{64,0},{128,64},{192,128},{256,192},{320,256},{384,320},{4... | collective-permute-start | bytes 589832 | tf_op jit(solution)/shard_map/ppermute | solution.py:346
  59.4 0.0 all-to-all-done.r_ref
  59.4 0.0 copy-done.5
  59.4 0.0 copy-done.6
  59.4 0.0 copy-done.7
  59.5 0.0 copy-done.4
  59.5 2.3 %there.1.f_ref = f32[512,512]{1,0:T(8,128)S(1)} custom-call(f32[32,64,128]{2,1,0:T(8,128)S(1)} %all-to-all-done.r_ref, bf16[256,512]{1,0:T(8,128)(2,1)S(1)} %copy-done.7, bf16[256,512]{1,0:T(8,128)(2,1)S(1)} %copy-done.6, bf16[256,512]{1,0:T(8,128)(2,1)S(1)} %copy-done.5, bf16[256,512]{1,0:T(8,128)(2,1)S(1)} %copy-done.4), custom_call_target="tpu_custom_call" | custom-call | flops 1610612736 | bytes 3145728 | tf_op jit(solution)/shard_map/there/pallas_call | solution.py:316
  61.7 0.0 copy-done.3
  61.7 0.0 copy-start.2
  61.8 1.9 %early.1.early_ref = f32[3,256,256]{2,1,0:T(8,128)S(1)} custom-call(s32[2]{0:T(128)S(1)} %pad_add_fusion.where_ref, f32[8,4,16,256]{3,2,1,0:T(8,128)S(1)} %all-gather.alike_ref, bf16[3,256,256]{2,1,0:T(8,128)(2,1)S(1)} %copy-done.3), custom_call_target="tpu_custom_call" | custom-call | flops 603979776 | bytes 1703944 | tf_op jit(solution)/shard_map/early/pallas_call | solution.py:316
  63.6 0.7 collective-permute-done.1.refs_1_
  64.3 0.0 collective-permute-done.refs_0_
  64.3 0.0 copy-done.2
  64.3 3.7 %back.1 = f32[32,64,128]{2,1,0:T(8,128)S(1)} custom-call(s32[2]{0:T(128)S(1)} %pad_add_fusion.where_ref, f32[512,512]{1,0:T(8,128)S(1)} %there.1.f_ref, f32[3,256,256]{2,1,0:T(8,128)S(1)} %early.1.early_ref, f32[5,4,16,256]{3,2,1,0:T(8,128)S(1)} %collective-permute-done.refs_0_, f32[3,4,16,256]{3,2,1,0:T(8,128)S(1)} %collective-permute-done.1.refs_1_, ...), custom_call_target="tpu_custom_call" | custom-call | flops 2013265920 | bytes 4849672 | tf_op jit(solution)/shard_map/back/pallas_call | solution.py:316
  68.0 0.0 copy-start
  68.0 0.0 copy-start.1
  68.0 38.2 %all_to_all.15 = f32[32,64,128]{2,1,0:T(8,128)S(1)} all-to-all(f32[32,64,128]{2,1,0:T(8,128)S(1)} %back.1), channel_id=1, replica_groups=mesh['z'=4,'parity'=2,'y_lo'=2,'gy'=8,'gz'=4] {'gy','gz'}, dimensions={0} | all-to-all | bytes 2097152 | tf_op jit(solution)/shard_map/all_to_all | solution.py:408
  106.2 0.0 copy-done
  106.2 0.0 copy-done.1
  106.2 1.6 %cells.1 = f32[2048,128]{1,0:T(8,128)} custom-call(f32[2048,128]{1,0:T(8,128)S(1)} %bitcast.9, bf16[128,128]{1,0:T(8,128)(2,1)S(1)} %copy-done.1, bf16[128,128]{1,0:T(8,128)(2,1)S(1)} %copy-done), custom_call_target="tpu_custom_call" | custom-call | flops 201326592 | bytes 2162688 | tf_op jit(solution)/shard_map/cells/pallas_call | solution.py:316
Async XLA Ops:
  1.7 19.7 %all-to-all-start.1 = ((f32[64,4,128]{2,1,0:T(4,128)}), f32[64,4,128]{2,1,0:T(4,128)S(1)}, u32[]{:S(2)}, u32[]{:S(2)}) async-start(f32[64,4,128]{2,1,0:T(4,128)} %bitcast.13), calls=%async_computation.1 | async-start | bytes 262144 | tf_op jit(solution)/shard_map/all_to_all | solution.py:343
  21.4 38.0 %all-to-all-start = ((f32[32,64,128]{2,1,0:T(8,128)}), f32[32,64,128]{2,1,0:T(8,128)S(1)}, u32[]{:S(2)}, u32[]{:S(2)}) async-start(f32[32,64,128]{2,1,0:T(8,128)} %bitcast.11), calls=%async_computation | async-start | bytes 2097152 | tf_op jit(solution)/shard_map/all_to_all | solution.py:373
  50.6 8.8 %copy-start.5 = (bf16[256,512]{1,0:T(8,128)(2,1)S(1)}, bf16[256,512]{1,0:T(8,128)(2,1)}, u32[]{:S(2)}) copy-start(bf16[256,512]{1,0:T(8,128)(2,1)} %constant.45.clone.rh.refs_5_) | copy-start | bytes 786436
  50.6 8.8 %copy-start.6 = (bf16[256,512]{1,0:T(8,128)(2,1)S(1)}, bf16[256,512]{1,0:T(8,128)(2,1)}, u32[]{:S(2)}) copy-start(bf16[256,512]{1,0:T(8,128)(2,1)} %constant.44.clone.ll.refs_4_) | copy-start | bytes 786436
  50.6 8.9 %copy-start.7 = (bf16[256,512]{1,0:T(8,128)(2,1)S(1)}, bf16[256,512]{1,0:T(8,128)(2,1)}, u32[]{:S(2)}) copy-start(bf16[256,512]{1,0:T(8,128)(2,1)} %constant.43.clone.lh.refs_3_) | copy-start | bytes 786436
  51.3 8.1 %copy-start.4 = (bf16[256,512]{1,0:T(8,128)(2,1)S(1)}, bf16[256,512]{1,0:T(8,128)(2,1)}, u32[]{:S(2)}) copy-start(bf16[256,512]{1,0:T(8,128)(2,1)} %constant.46.clone.rl.refs_6_) | copy-start | bytes 786436
  51.3 13.0 %collective-permute-start = (f32[5,4,16,256]{3,2,1,0:T(8,128)}, f32[5,4,16,256]{3,2,1,0:T(8,128)S(1)}, u32[]{:S(2)}, u32[]{:S(2)}) collective-permute-start(f32[5,4,16,256]{3,2,1,0:T(8,128)} %slice.8), channel_id=1, source_target_pairs={{0,64},{64,128},{128,192},{192,256},{256,320},{320,384},{384,448},... | collective-permute-start | bytes 983048 | tf_op jit(solution)/shard_map/ppermute | solution.py:346
  55.6 6.1 %copy-start.3 = (bf16[3,256,256]{2,1,0:T(8,128)(2,1)S(1)}, bf16[3,256,256]{2,1,0:T(8,128)(2,1)}, u32[]{:S(2)}) copy-start(bf16[3,256,256]{2,1,0:T(8,128)(2,1)} %constant.48.clone.table_ref) | copy-start | bytes 1179652
  55.6 8.7 %collective-permute-start.1 = (f32[3,4,16,256]{3,2,1,0:T(8,128)}, f32[3,4,16,256]{3,2,1,0:T(8,128)S(1)}, u32[]{:S(2)}, u32[]{:S(2)}) collective-permute-start(f32[3,4,16,256]{3,2,1,0:T(8,128)} %slice.9), channel_id=1, source_target_pairs={{0,448},{64,0},{128,64},{192,128},{256,192},{320,256},{384,320},{4... | collective-permute-start | bytes 589832 | tf_op jit(solution)/shard_map/ppermute | solution.py:346
  61.7 2.6 %copy-start.2 = (bf16[3,256,256]{2,1,0:T(8,128)(2,1)S(1)}, bf16[3,256,256]{2,1,0:T(8,128)(2,1)}, u32[]{:S(2)}) copy-start(bf16[3,256,256]{2,1,0:T(8,128)(2,1)} %constant.49.clone.refs_2_) | copy-start | bytes 1179652
  68.0 38.3 %copy-start = (bf16[128,128]{1,0:T(8,128)(2,1)S(1)}, bf16[128,128]{1,0:T(8,128)(2,1)}, u32[]{:S(2)}) copy-start(bf16[128,128]{1,0:T(8,128)(2,1)} %constant.42.clone.low_ref) | copy-start | bytes 98308
  68.0 38.3 %copy-start.1 = (bf16[128,128]{1,0:T(8,128)(2,1)S(1)}, bf16[128,128]{1,0:T(8,128)(2,1)}, u32[]{:S(2)}) copy-start(bf16[128,128]{1,0:T(8,128)(2,1)} %constant.41.clone.high_ref) | copy-start | bytes 98308
